TPU v7x, 32 devices: a whole 2x2x4 slice. The times are simulated.
32 devices in a mesh: gx: 8 (over z, x), gy: 4 (over y, core).
Axes of the slice: x: 2, y: 2, z: 4, core: 2. Of those that a mesh axis runs over, the one named last changes fastest.
Arguments:
- velocity: float32 [3, 64, 64, 128], P(None, 'gx', 'gy'), may hold values from -6 to 6
- stress: float32 [6, 64, 64, 128], P(None, 'gx', 'gy'), may hold values from -6 to 6
- lame_first: float32 [64, 64, 128], P('gx', 'gy'), may hold values from 0.5 to 1.5
- shear_modulus: float32 [64, 64, 128], P('gx', 'gy'), may hold values from 0.3 to 1
- buoyancy: float32 [64, 64, 128], P('gx', 'gy'), may hold values from 0.5 to 1
- forward_strain: bfloat16 [12, 64, 64, 128], P(None, 'gx', 'gy'), may hold values from -6 to 6
- lame_accum: float32 [64, 64, 128], P('gx', 'gy'), may hold values from -6 to 6
- shear_accum: float32 [64, 64, 128], P('gx', 'gy'), may hold values from -6 to 6
- residuals: bfloat16 [1024, 4096], P(('gx', 'gy')), may hold values from -24 to 24
- station_cell: int32 [1024], P(('gx', 'gy')), may hold values from 0 to 127
- station_pairs: int32 [4096, 2], replicated, may hold values from 0 to 1023, as said below
Outputs:
- new_velocity: float32 [3, 64, 64, 128], P(None, 'gx', 'gy')
- new_stress: float32 [6, 64, 64, 128], P(None, 'gx', 'gy')
- lame_kernel: float32 [64, 64, 128], P('gx', 'gy')
- shear_kernel: float32 [64, 64, 128], P('gx', 'gy')
- adjoint_source: float32 [1024, 4096], P(('gx', 'gy'))
Inputs may be any that keep to these rules, and one draw needn't show every extreme that they name: station_cell[s] numbers the surface cell x * 16 + y of station s within the block of the device that holds station s. `station_pairs`: stations s * 32 to (s + 1) * 32 - 1 are held by device s of gx+gy. The first station of pair p is held by device p // 128. Among the 128 pairs of one device, at most 8 have a second station held by any one device; some may have none. Some device's stations are the second station of exactly 8 pairs of every device.
All inputs are finite; a program needn't handle non-finite values.
Results may differ from a plain program's by a relative error of at most 0.0017.
Values may be sent and summed in bfloat16 or wider, within the bound.
A program may use at most 64 MiB of HBM per device.

v0:
```python
import jax
import jax.numpy as jnp
from jax import lax
from jax.sharding import PartitionSpec as P

near_weight = 9.0 / 8.0
far_weight = -1.0 / 24.0
time_step = 0.25
epsilon = 1e-06


def with_halo(block, sides, width):
    for axis, dim in sides:
        count = lax.axis_size(axis)
        forward = [(i, i + 1) for i in range(count - 1)]
        backward = [(target, source) for source, target in forward]
        low = lax.ppermute(
            lax.slice_in_dim(block, block.shape[dim] - width, None, axis=dim), axis, forward
        )
        high = lax.ppermute(lax.slice_in_dim(block, 0, width, axis=dim), axis, backward)
        block = jnp.concatenate([low, block, high], axis=dim)
    return block


def shifted(padded, start, length, axis):
    return lax.slice_in_dim(padded, start, start + length, axis=axis)


def backward_diff(padded, length, axis):
    return near_weight * (
        shifted(padded, 2, length, axis) - shifted(padded, 1, length, axis)
    ) + far_weight * (shifted(padded, 3, length, axis) - shifted(padded, 0, length, axis))


def forward_diff(padded, length, axis):
    return near_weight * (
        shifted(padded, 3, length, axis) - shifted(padded, 2, length, axis)
    ) + far_weight * (shifted(padded, 4, length, axis) - shifted(padded, 1, length, axis))


def pair_terms(first_rows, second_rows):
    first_vals = first_rows.astype(jnp.float32)
    second_vals = second_rows.astype(jnp.float32)
    first_vals = first_vals / jnp.sqrt(
        jnp.mean(first_vals * first_vals, axis=1, keepdims=True) + epsilon
    )
    second_vals = second_vals / jnp.sqrt(
        jnp.mean(second_vals * second_vals, axis=1, keepdims=True) + epsilon
    )
    corr = jnp.mean(first_vals * second_vals, axis=1, keepdims=True)
    return (
        (second_vals - corr * first_vals).astype(jnp.bfloat16),
        (first_vals - corr * second_vals).astype(jnp.bfloat16),
    )


def contract(hits, rows):
    return lax.dot_general(hits, rows, (((0,), (0,)), ((), ())), preferred_element_type=jnp.float32)


def route_slots(rows):
    return lax.all_to_all(rows, ("gx", "gy"), split_axis=0, concat_axis=0, tiled=True)


def stress_sides(stress):
    cells_first = stress.shape[1]
    cells_second = stress.shape[2]
    wide_stress = with_halo(stress, (("gx", 1), ("gy", 2)), 2)
    first_part = wide_stress[:, :, 2 : 2 + cells_second, :]
    second_part = wide_stress[:, 2 : 2 + cells_first, :, :]
    return (
        (first_part[0], first_part[3], first_part[4]),
        (second_part[1], second_part[3], second_part[5]),
    )


def motion_sides(moved):
    cells_first = moved.shape[1]
    cells_second = moved.shape[2]
    wide_motion = with_halo(moved, (("gx", 1), ("gy", 2)), 2)
    return (wide_motion[:, :, 2 : 2 + cells_second, :], wide_motion[:, 2 : 2 + cells_first, :, :])


def advance(
    velocity,
    stress,
    lame_first,
    shear_modulus,
    buoyancy,
    strain_now,
    surface,
    lame_kernel,
    shear_kernel,
):
    cells_first = velocity.shape[1]
    cells_second = velocity.shape[2]
    cells_third = velocity.shape[3]
    across_stress, along_stress = stress_sides(stress)
    stress_third = jnp.pad(stress, ((0, 0), (0, 0), (0, 0), (2, 2)))
    force_first = (
        forward_diff(across_stress[0], cells_first, 0)
        + backward_diff(along_stress[1], cells_second, 1)
        + backward_diff(stress_third[4], cells_third, 2)
    )
    force_second = (
        backward_diff(across_stress[1], cells_first, 0)
        + forward_diff(along_stress[0], cells_second, 1)
        + backward_diff(stress_third[5], cells_third, 2)
    )
    force_third = (
        backward_diff(across_stress[2], cells_first, 0)
        + backward_diff(along_stress[2], cells_second, 1)
        + forward_diff(stress_third[2], cells_third, 2)
    )
    force_third = force_third.at[:, :, 0].add(surface)
    moved = velocity + time_step * buoyancy[None] * jnp.stack(
        [force_first, force_second, force_third]
    )
    motion_first, motion_second = motion_sides(moved)
    motion_third = jnp.pad(moved, ((0, 0), (0, 0), (0, 0), (2, 2)))
    rate_first = backward_diff(motion_first[0], cells_first, 0)
    rate_second = backward_diff(motion_second[1], cells_second, 1)
    rate_third = backward_diff(motion_third[2], cells_third, 2)
    shear_one = forward_diff(motion_second[0], cells_second, 1) + forward_diff(
        motion_first[1], cells_first, 0
    )
    shear_two = forward_diff(motion_third[0], cells_third, 2) + forward_diff(
        motion_first[2], cells_first, 0
    )
    shear_three = forward_diff(motion_third[1], cells_third, 2) + forward_diff(
        motion_second[2], cells_second, 1
    )
    dilation = rate_first + rate_second + rate_third
    grown = stress + time_step * jnp.stack(
        [
            lame_first * dilation + 2.0 * shear_modulus * rate_first,
            lame_first * dilation + 2.0 * shear_modulus * rate_second,
            lame_first * dilation + 2.0 * shear_modulus * rate_third,
            shear_modulus * shear_one,
            shear_modulus * shear_two,
            shear_modulus * shear_three,
        ]
    )
    strain_vals = strain_now.astype(jnp.float32)
    lame_kernel = (
        lame_kernel + time_step * (strain_vals[0] + strain_vals[1] + strain_vals[2]) * dilation
    )
    shear_kernel = shear_kernel + 2.0 * time_step * (
        strain_vals[0] * rate_first
        + strain_vals[1] * rate_second
        + strain_vals[2] * rate_third
        + strain_vals[3] * shear_one
        + strain_vals[4] * shear_two
        + strain_vals[5] * shear_three
    )
    return (moved, grown, lame_kernel, shear_kernel)


def shards(
    velocity,
    stress,
    lame_first,
    shear_modulus,
    buoyancy,
    forward_strain,
    lame_accum,
    shear_accum,
    residuals,
    station_cell,
    station_pairs,
):
    stations_here = residuals.shape[0]
    samples = residuals.shape[1]
    devices = lax.axis_size(("gx", "gy"))
    pair_rows = station_pairs.shape[0] // devices
    slot_count = 2 * pair_rows
    capacity = slot_count // devices
    device_index = lax.axis_index(("gx", "gy"))
    own_pairs = lax.dynamic_slice_in_dim(station_pairs, device_index * pair_rows, pair_rows, 0)
    first_local = own_pairs[:, 0] - device_index * stations_here
    owner_device = own_pairs[:, 1] // stations_here
    order_index = jnp.arange(pair_rows)
    earlier = (owner_device[:, None] == owner_device[None, :]) & (
        order_index[None, :] < order_index[:, None]
    )
    slot_index = owner_device * capacity + jnp.sum(earlier.astype(jnp.int32), axis=1)
    blocks = station_pairs.reshape(devices, pair_rows, 2)
    mine_mask = (blocks[:, :, 1] // stations_here == device_index).astype(jnp.int32)
    before = jnp.cumsum(mine_mask, axis=1) - mine_mask
    matches = (
        (mine_mask[:, :, None] > 0) & (before[:, :, None] == jnp.arange(capacity)[None, None, :])
    ).astype(jnp.int32)
    wanted = (blocks[:, :, 1] % stations_here)[:, :, None]
    found = jnp.sum(matches, axis=1)
    picked = jnp.sum(matches * wanted, axis=1)
    asked_ids = jnp.where(found > 0, picked, -1).reshape(slot_count)
    station_ids = jnp.arange(stations_here)
    first_hits = (first_local[:, None] == station_ids[None, :]).astype(jnp.bfloat16)
    asked_hits = (asked_ids[:, None] == station_ids[None, :]).astype(jnp.bfloat16)
    first_rows = residuals[first_local]
    local_rows = jnp.where(
        asked_ids[:, None] >= 0, residuals[jnp.maximum(asked_ids, 0)], jnp.zeros((), jnp.bfloat16)
    )
    carried = jnp.zeros((slot_count, samples), jnp.bfloat16).at[slot_index].set(first_rows)
    arrived = route_slots(carried)
    toward_first, toward_second = pair_terms(arrived, local_rows)
    returned = route_slots(toward_first)
    adjoint = contract(first_hits, returned[slot_index]) + contract(asked_hits, toward_second)
    cells_first = velocity.shape[1]
    cells_second = velocity.shape[2]
    step_count = forward_strain.shape[0] // 6
    cells_hit = (station_cell[:, None] == jnp.arange(cells_first * cells_second)[None, :]).astype(
        jnp.float32
    )
    surfaces = jnp.stack(
        [
            jnp.sum(cells_hit * adjoint[:, samples - 1 - window_step][:, None], axis=0).reshape(
                cells_first, cells_second
            )
            for window_step in range(step_count)
        ]
    )
    for window_step in range(step_count):
        strain_now = forward_strain[6 * window_step : 6 * window_step + 6]
        velocity, stress, lame_accum, shear_accum = advance(
            velocity,
            stress,
            lame_first,
            shear_modulus,
            buoyancy,
            strain_now,
            surfaces[window_step],
            lame_accum,
            shear_accum,
        )
    return (velocity, stress, lame_accum, shear_accum, adjoint)


def solution(mesh):
    return jax.shard_map(
        shards,
        mesh=mesh,
        in_specs=(
            P(None, "gx", "gy", None),
            P(None, "gx", "gy", None),
            P("gx", "gy", None),
            P("gx", "gy", None),
            P("gx", "gy", None),
            P(None, "gx", "gy", None),
            P("gx", "gy", None),
            P("gx", "gy", None),
            P(("gx", "gy"), None),
            P(("gx", "gy")),
            P(),
        ),
        out_specs=(
            P(None, "gx", "gy", None),
            P(None, "gx", "gy", None),
            P("gx", "gy", None),
            P("gx", "gy", None),
            P(("gx", "gy"), None),
        ),
        check_vma=False,
    )
```

profile of v0, /device:TPU:0, one launch (start us, length us, event | category | flops | bytes accessed | tf_op | source)
XLA Modules:
  0.0 196.6 jit_solution(1701139880624806756)
XLA Ops:
  1.6 6.7 %scatter_custom_fusion = bf16[256,4096]{1,0:T(8,128)(2,1)} fusion(s32[128]{0:T(128)S(1)} %fusion.227, bf16[32,4096]{1,0:T(8,128)(2,1)S(1)} %copy-done, s32[1024]{0:T(1024)S(1)} %pad_clamp_fusion.1, bf16[]{:T(256)} %constant.138.clone.1), kind=kCustom, calls=%fused_computation.41 | custom fusion | bytes 2097154 | tf_op jit(solution)/shard_map/scatter | solution.py:204
  8.3 7.5 %all-to-all-start = ((bf16[32,8,4096]{2,1,0:T(8,128)(2,1)}), bf16[32,8,4096]{2,1,0:T(8,128)(2,1)S(1)}, u32[]{:S(2)}, u32[]{:S(2)}) async-start(bf16[32,8,4096]{2,1,0:T(8,128)(2,1)} %bitcast.272), calls=%async_computation | async-start | bytes 4194304 | tf_op jit(solution)/shard_map/all_to_all | solution.py:62
  15.9 2.9 %copy.343 = s32[32,128,1]{2,0,1:T(8,128)} copy(s32[32,128,1]{1,0,2:T(8,128)S(1)} %slice.1079) | data formatting | bytes 32768
  18.7 3.7 %add_select_fusion = s32[32,128,1]{2,0,1:T(8,128)} fusion(s32[32,128,1]{2,0,1:T(8,128)} %copy.343), kind=kLoop, calls=%fused_computation.23 | loop fusion | flops 45056 | bytes 32768 | tf_op jit(solution)/shard_map/jit(remainder)/select_n | solution.py:193
  22.4 2.7 %copy.338 = s32[32,128,1]{1,0,2:T(8,128)S(1)} copy(s32[32,128,1]{2,0,1:T(8,128)} %add_select_fusion) | data formatting | bytes 32768 | tf_op jit(solution)/shard_map/jit(remainder)/select_n | solution.py:193
  25.1 3.8 %convert_compare_fusion = (pred[32,128,1]{2,0,1:T(8,128)(4,1)}, pred[32,128,1]{2,0,1:T(8,128)(4,1)S(1)}) fusion(s32[]{:T(128)S(6)} %add.397, s32[32,128,1]{2,0,1:T(8,128)} %copy.343), kind=kLoop, calls=%fused_computation.22 | loop fusion | flops 73728 | bytes 24580 | tf_op jit(solution)/shard_map/gt | solution.py:191
  32.9 2.7 %copy.337 = s32[32,128,1]{1,0,2:T(8,128)S(1)} copy(s32[32,128,1]{2,0,1:T(8,128)} %convert_subtract_fusion) | data formatting | bytes 32768 | tf_op jit(solution)/shard_map/sub | solution.py:189
  36.9 3.2 %gather_fusion = bf16[256,4096]{1,0:T(8,128)(2,1)} fusion(bf16[32,4096]{1,0:T(8,128)(2,1)S(1)} %copy-done, s32[1024]{0:T(1024)S(1)} %pad_clamp_fusion.2), kind=kCustom, calls=%fused_computation | custom fusion | bytes 4195328 | tf_op jit(solution)/shard_map/gather | solution.py:202
  42.5 21.9 %all-to-all-done = bf16[32,8,4096]{2,1,0:T(8,128)(2,1)S(1)} async-done(((bf16[32,8,4096]{2,1,0:T(8,128)(2,1)}), bf16[32,8,4096]{2,1,0:T(8,128)(2,1)S(1)}, u32[]{:S(2)}, u32[]{:S(2)}) %all-to-all-start) | async-done | bytes 2097184 | tf_op jit(solution)/shard_map/all_to_all | solution.py:62
  67.9 2.8 %subtract_convert_fusion = bf16[32,8,4096]{2,1,0:T(8,128)(2,1)} fusion(bf16[32,8,4096]{2,1,0:T(8,128)(2,1)S(1)} %all-to-all-done, f32[32,8]{1,0:T(8,128)S(1)} %broadcast_multiply_fusion.1, f32[32,8]{1,0:T(8,128)S(1)} %add_sqrt_fusion, f32[32,8]{1,0:T(8,128)S(1)} %sqrt.25, bf16[256,4096]{1,0:T(8,128)(2,1)S(1)} %copy-done.2, ...), kind=kLoop, calls=%fused_computation.16 | loop fusion | flops 8388608 | bytes 6294784 | tf_op jit(solution)/shard_map/convert_element_type | solution.py:52
  70.7 4.1 %all-to-all-start.1 = ((bf16[32,8,4096]{2,1,0:T(8,128)(2,1)}), bf16[32,8,4096]{2,1,0:T(8,128)(2,1)S(1)}, u32[]{:S(2)}, u32[]{:S(2)}) async-start(bf16[32,8,4096]{2,1,0:T(8,128)(2,1)} %subtract_convert_fusion), calls=%async_computation.1 | async-start | bytes 4194304 | tf_op jit(solution)/shard_map/all_to_all | solution.py:62
  76.1 4.6 %collective-permute-start.1 = (f32[6,2,16,128]{3,2,1,0:T(8,128)S(1)}, f32[6,2,16,128]{3,2,1,0:T(8,128)S(1)}, u32[]{:S(2)}, u32[]{:S(2)}) collective-permute-start(f32[6,2,16,128]{3,2,1,0:T(8,128)S(1)} %get-tuple-element.103), channel_id=1, source_target_pairs={{0,4},{4,8},{8,12},{12,16},{16,20},{20,24},{24,28},{1,5},{5,9},{9,... | collective-permute-start | bytes 294920 | tf_op jit(solution)/shard_map/ppermute | solution.py:17
  80.9 11.4 %collective-permute-done.1 = f32[6,2,16,128]{3,2,1,0:T(8,128)S(1)} collective-permute-done((f32[6,2,16,128]{3,2,1,0:T(8,128)S(1)}, f32[6,2,16,128]{3,2,1,0:T(8,128)S(1)}, u32[]{:S(2)}, u32[]{:S(2)}) %collective-permute-start.1) | collective-permute-done | bytes 98336 | tf_op jit(solution)/shard_map/ppermute | solution.py:17
  100.1 4.3 %fusion.10 = f32[32,4096]{1,0:T(8,128)} fusion(bf16[32,8,4096]{2,1,0:T(8,128)(2,1)} %copy-done.1, f32[256]{0:T(256)S(1)} %add_sqrt_fusion.1, f32[256]{0:T(256)S(1)} %div.92, f32[256]{0:T(256)S(1)} %sqrt.27, bf16[256,4096]{1,0:T(8,128)(2,1)} %gather_fusion, pred[256]{0:T(512)(128)(4,1)S(1)} %broadcast_compare_fusion.1, s32[256]{0:T(256)S(1)} %select_n.79), kind=kOutput, calls=%fused_computation.33 | convolution fusion | flops 75505664 | bytes 4722944 | tf_op jit(solution)/shard_map/dot_general | solution.py:58
  104.4 19.6 %all-to-all-done.1 = bf16[32,8,4096]{2,1,0:T(8,128)(2,1)S(1)} async-done(((bf16[32,8,4096]{2,1,0:T(8,128)(2,1)}), bf16[32,8,4096]{2,1,0:T(8,128)(2,1)S(1)}, u32[]{:S(2)}, u32[]{:S(2)}) %all-to-all-start.1) | async-done | bytes 2097184 | tf_op jit(solution)/shard_map/all_to_all | solution.py:62
  128.7 2.8 %collective-permute-start.4 = (f32[3,2,16,128]{3,2,1,0:T(8,128)S(1)}, f32[3,2,16,128]{3,2,1,0:T(8,128)S(1)}, u32[]{:S(2)}, u32[]{:S(2)}) collective-permute-start(f32[3,2,16,128]{3,2,1,0:T(8,128)S(1)} %get-tuple-element.122), channel_id=1, source_target_pairs={{0,4},{4,8},{8,12},{12,16},{16,20},{20,24},{24,28},{1,5},{5,9},{9,... | collective-permute-start | bytes 147464 | tf_op jit(solution)/shard_map/ppermute | solution.py:17
  133.3 5.3 %collective-permute-done.5 = f32[3,2,16,128]{3,2,1,0:T(8,128)S(1)} collective-permute-done((f32[3,2,16,128]{3,2,1,0:T(8,128)S(1)}, f32[3,2,16,128]{3,2,1,0:T(8,128)S(1)}, u32[]{:S(2)}, u32[]{:S(2)}) %collective-permute-start.5) | collective-permute-done | bytes 49184 | tf_op jit(solution)/shard_map/ppermute | solution.py:20
  138.6 3.8 %collective-permute-start.6 = (f32[3,12,2,128]{3,2,1,0:T(2,128)S(1)}, f32[3,12,2,128]{3,2,1,0:T(2,128)S(1)}, u32[]{:S(2)}, u32[]{:S(2)}) collective-permute-start(f32[3,12,2,128]{3,2,1,0:T(2,128)S(1)} %get-tuple-element.112), channel_id=1, source_target_pairs={{0,1},{1,2},{2,3},{4,5},{5,6},{6,7},{8,9},{9,10},{10,11},{12,13},{... | collective-permute-start | bytes 110600 | tf_op jit(solution)/shard_map/ppermute | solution.py:17
  146.7 14.2 %collective-permute-start.9 = (f32[6,2,16,128]{3,2,1,0:T(8,128)S(1)}, f32[6,2,16,128]{3,2,1,0:T(8,128)S(1)}, u32[]{:S(2)}, u32[]{:S(2)}) collective-permute-start(f32[6,2,16,128]{3,2,1,0:T(8,128)S(1)} %get-tuple-element.94), channel_id=1, source_target_pairs={{0,4},{4,8},{8,12},{12,16},{16,20},{20,24},{24,28},{1,5},{5,9},{9,... | collective-permute-start | bytes 294920 | tf_op jit(solution)/shard_map/ppermute | solution.py:17
  163.2 4.4 %collective-permute-done.8 = f32[6,2,16,128]{3,2,1,0:T(8,128)S(1)} collective-permute-done((f32[6,2,16,128]{3,2,1,0:T(8,128)S(1)}, f32[6,2,16,128]{3,2,1,0:T(8,128)S(1)}, u32[]{:S(2)}, u32[]{:S(2)}) %collective-permute-start.8) | collective-permute-done | bytes 98336 | tf_op jit(solution)/shard_map/ppermute | solution.py:20
  167.7 3.4 %collective-permute-start.10 = (f32[6,12,2,128]{3,2,1,0:T(2,128)S(1)}, f32[6,12,2,128]{3,2,1,0:T(2,128)S(1)}, u32[]{:S(2)}, u32[]{:S(2)}) collective-permute-start(f32[6,12,2,128]{3,2,1,0:T(2,128)S(1)} %get-tuple-element.85), channel_id=1, source_target_pairs={{0,1},{1,2},{2,3},{4,5},{5,6},{6,7},{8,9},{9,10},{10,11},{12,13},{... | collective-permute-start | bytes 221192 | tf_op jit(solution)/shard_map/ppermute | solution.py:17
  175.6 4.8 %collective-permute-start.12 = (f32[3,2,16,128]{3,2,1,0:T(8,128)S(1)}, f32[3,2,16,128]{3,2,1,0:T(8,128)S(1)}, u32[]{:S(2)}, u32[]{:S(2)}) collective-permute-start(f32[3,2,16,128]{3,2,1,0:T(8,128)S(1)} %get-tuple-element.117), channel_id=1, source_target_pairs={{0,4},{4,8},{8,12},{12,16},{16,20},{20,24},{24,28},{1,5},{5,9},{9,... | collective-permute-start | bytes 147464 | tf_op jit(solution)/shard_map/ppermute | solution.py:17
  182.2 4.3 %collective-permute-done.13 = f32[3,2,16,128]{3,2,1,0:T(8,128)S(1)} collective-permute-done((f32[3,2,16,128]{3,2,1,0:T(8,128)S(1)}, f32[3,2,16,128]{3,2,1,0:T(8,128)S(1)}, u32[]{:S(2)}, u32[]{:S(2)}) %collective-permute-start.13) | collective-permute-done | bytes 49184 | tf_op jit(solution)/shard_map/ppermute | solution.py:20
  186.5 3.8 %collective-permute-start.14 = (f32[3,12,2,128]{3,2,1,0:T(2,128)S(1)}, f32[3,12,2,128]{3,2,1,0:T(2,128)S(1)}, u32[]{:S(2)}, u32[]{:S(2)}) collective-permute-start(f32[3,12,2,128]{3,2,1,0:T(2,128)S(1)} %get-tuple-element.110), channel_id=1, source_target_pairs={{0,1},{1,2},{2,3},{4,5},{5,6},{6,7},{8,9},{9,10},{10,11},{12,13},{... | collective-permute-start | bytes 110600 | tf_op jit(solution)/shard_map/ppermute | solution.py:17
  (133 shorter events, 46.7 us)
Async XLA Ops:
  8.3 56.1 %all-to-all-start = ((bf16[32,8,4096]{2,1,0:T(8,128)(2,1)}), bf16[32,8,4096]{2,1,0:T(8,128)(2,1)S(1)}, u32[]{:S(2)}, u32[]{:S(2)}) async-start(bf16[32,8,4096]{2,1,0:T(8,128)(2,1)} %bitcast.272), calls=%async_computation | async-start | bytes 4194304 | tf_op jit(solution)/shard_map/all_to_all | solution.py:62
  70.7 10.0 %copy-start.12 = (f32[8,16,128]{2,1,0:T(8,128)S(1)}, f32[8,16,128]{2,1,0:T(8,128)}, u32[]{:S(2)}) copy-start(f32[8,16,128]{2,1,0:T(8,128)} %param.19) | copy-start | bytes 196612
  70.7 53.4 %all-to-all-start.1 = ((bf16[32,8,4096]{2,1,0:T(8,128)(2,1)}), bf16[32,8,4096]{2,1,0:T(8,128)(2,1)S(1)}, u32[]{:S(2)}, u32[]{:S(2)}) async-start(bf16[32,8,4096]{2,1,0:T(8,128)(2,1)} %subtract_convert_fusion), calls=%async_computation.1 | async-start | bytes 4194304 | tf_op jit(solution)/shard_map/all_to_all | solution.py:62
  74.8 19.5 %collective-permute-start = (f32[6,2,16,128]{3,2,1,0:T(8,128)S(1)}, f32[6,2,16,128]{3,2,1,0:T(8,128)S(1)}, u32[]{:S(2)}, u32[]{:S(2)}) collective-permute-start(f32[6,2,16,128]{3,2,1,0:T(8,128)S(1)} %get-tuple-element.102), channel_id=1, source_target_pairs={{4,0},{8,4},{12,8},{16,12},{20,16},{24,20},{28,24},{5,1},{9,5},{13... | collective-permute-start | bytes 294920 | tf_op jit(solution)/shard_map/ppermute | solution.py:20
  76.1 16.2 %collective-permute-start.1 = (f32[6,2,16,128]{3,2,1,0:T(8,128)S(1)}, f32[6,2,16,128]{3,2,1,0:T(8,128)S(1)}, u32[]{:S(2)}, u32[]{:S(2)}) collective-permute-start(f32[6,2,16,128]{3,2,1,0:T(8,128)S(1)} %get-tuple-element.103), channel_id=1, source_target_pairs={{0,4},{4,8},{8,12},{12,16},{16,20},{20,24},{24,28},{1,5},{5,9},{9,... | collective-permute-start | bytes 294920 | tf_op jit(solution)/shard_map/ppermute | solution.py:17
  94.4 2.6 %collective-permute-start.2 = (f32[6,12,2,128]{3,2,1,0:T(2,128)S(1)}, f32[6,12,2,128]{3,2,1,0:T(2,128)S(1)}, u32[]{:S(2)}, u32[]{:S(2)}) collective-permute-start(f32[6,12,2,128]{3,2,1,0:T(2,128)S(1)} %get-tuple-element.87), channel_id=1, source_target_pairs={{0,1},{1,2},{2,3},{4,5},{5,6},{6,7},{8,9},{9,10},{10,11},{12,13},{... | collective-permute-start | bytes 221192 | tf_op jit(solution)/shard_map/ppermute | solution.py:17
  95.7 3.8 %collective-permute-start.3 = (f32[6,12,2,128]{3,2,1,0:T(2,128)S(1)}, f32[6,12,2,128]{3,2,1,0:T(2,128)S(1)}, u32[]{:S(2)}, u32[]{:S(2)}) collective-permute-start(f32[6,12,2,128]{3,2,1,0:T(2,128)S(1)} %get-tuple-element.88), channel_id=1, source_target_pairs={{1,0},{2,1},{3,2},{5,4},{6,5},{7,6},{9,8},{10,9},{11,10},{13,12},{... | collective-permute-start | bytes 221192 | tf_op jit(solution)/shard_map/ppermute | solution.py:20
  126.2 19.9 %copy-start.3 = (f32[8,16,128]{2,1,0:T(8,128)S(1)}, f32[8,16,128]{2,1,0:T(8,128)}, u32[]{:S(2)}) copy-start(f32[8,16,128]{2,1,0:T(8,128)} %param.18) | copy-start | bytes 196612
  126.2 19.9 %copy-start.9 = (f32[8,16,128]{2,1,0:T(8,128)S(1)}, f32[8,16,128]{2,1,0:T(8,128)}, u32[]{:S(2)}) copy-start(f32[8,16,128]{2,1,0:T(8,128)} %param.17) | copy-start | bytes 196612
  128.0 18.3 %copy-start.7 = (f32[32,4096]{1,0:T(8,128)}, f32[32,4096]{1,0:T(8,128)S(1)}, u32[]{:S(2)}) copy-start(f32[32,4096]{1,0:T(8,128)S(1)} %convolution_add_fusion) | copy-start | bytes 1572868
  128.7 4.6 %collective-permute-start.4 = (f32[3,2,16,128]{3,2,1,0:T(8,128)S(1)}, f32[3,2,16,128]{3,2,1,0:T(8,128)S(1)}, u32[]{:S(2)}, u32[]{:S(2)}) collective-permute-start(f32[3,2,16,128]{3,2,1,0:T(8,128)S(1)} %get-tuple-element.122), channel_id=1, source_target_pairs={{0,4},{4,8},{8,12},{12,16},{16,20},{20,24},{24,28},{1,5},{5,9},{9,... | collective-permute-start | bytes 147464 | tf_op jit(solution)/shard_map/ppermute | solution.py:17
  131.6 7.0 %collective-permute-start.5 = (f32[3,2,16,128]{3,2,1,0:T(8,128)S(1)}, f32[3,2,16,128]{3,2,1,0:T(8,128)S(1)}, u32[]{:S(2)}, u32[]{:S(2)}) collective-permute-start(f32[3,2,16,128]{3,2,1,0:T(8,128)S(1)} %get-tuple-element.123), channel_id=1, source_target_pairs={{4,0},{8,4},{12,8},{16,12},{20,16},{24,20},{28,24},{5,1},{9,5},{13... | collective-permute-start | bytes 147464 | tf_op jit(solution)/shard_map/ppermute | solution.py:20
  138.6 5.2 %collective-permute-start.6 = (f32[3,12,2,128]{3,2,1,0:T(2,128)S(1)}, f32[3,12,2,128]{3,2,1,0:T(2,128)S(1)}, u32[]{:S(2)}, u32[]{:S(2)}) collective-permute-start(f32[3,12,2,128]{3,2,1,0:T(2,128)S(1)} %get-tuple-element.112), channel_id=1, source_target_pairs={{0,1},{1,2},{2,3},{4,5},{5,6},{6,7},{8,9},{9,10},{10,11},{12,13},{... | collective-permute-start | bytes 110600 | tf_op jit(solution)/shard_map/ppermute | solution.py:17
  142.4 3.7 %collective-permute-start.7 = (f32[3,12,2,128]{3,2,1,0:T(2,128)S(1)}, f32[3,12,2,128]{3,2,1,0:T(2,128)S(1)}, u32[]{:S(2)}, u32[]{:S(2)}) collective-permute-start(f32[3,12,2,128]{3,2,1,0:T(2,128)S(1)} %get-tuple-element.113), channel_id=1, source_target_pairs={{1,0},{2,1},{3,2},{5,4},{6,5},{7,6},{9,8},{10,9},{11,10},{13,12},{... | collective-permute-start | bytes 110600 | tf_op jit(solution)/shard_map/ppermute | solution.py:20
  146.7 16.4 %collective-permute-start.9 = (f32[6,2,16,128]{3,2,1,0:T(8,128)S(1)}, f32[6,2,16,128]{3,2,1,0:T(8,128)S(1)}, u32[]{:S(2)}, u32[]{:S(2)}) collective-permute-start(f32[6,2,16,128]{3,2,1,0:T(8,128)S(1)} %get-tuple-element.94), channel_id=1, source_target_pairs={{0,4},{4,8},{8,12},{12,16},{16,20},{20,24},{24,28},{1,5},{5,9},{9,... | collective-permute-start | bytes 294920 | tf_op jit(solution)/shard_map/ppermute | solution.py:17
  161.0 6.6 %collective-permute-start.8 = (f32[6,2,16,128]{3,2,1,0:T(8,128)S(1)}, f32[6,2,16,128]{3,2,1,0:T(8,128)S(1)}, u32[]{:S(2)}, u32[]{:S(2)}) collective-permute-start(f32[6,2,16,128]{3,2,1,0:T(8,128)S(1)} %get-tuple-element.95), channel_id=1, source_target_pairs={{4,0},{8,4},{12,8},{16,12},{20,16},{24,20},{28,24},{5,1},{9,5},{13... | collective-permute-start | bytes 294920 | tf_op jit(solution)/shard_map/ppermute | solution.py:20
  167.7 4.9 %collective-permute-start.10 = (f32[6,12,2,128]{3,2,1,0:T(2,128)S(1)}, f32[6,12,2,128]{3,2,1,0:T(2,128)S(1)}, u32[]{:S(2)}, u32[]{:S(2)}) collective-permute-start(f32[6,12,2,128]{3,2,1,0:T(2,128)S(1)} %get-tuple-element.85), channel_id=1, source_target_pairs={{0,1},{1,2},{2,3},{4,5},{5,6},{6,7},{8,9},{9,10},{10,11},{12,13},{... | collective-permute-start | bytes 221192 | tf_op jit(solution)/shard_map/ppermute | solution.py:17
  171.1 3.8 %collective-permute-start.11 = (f32[6,12,2,128]{3,2,1,0:T(2,128)S(1)}, f32[6,12,2,128]{3,2,1,0:T(2,128)S(1)}, u32[]{:S(2)}, u32[]{:S(2)}) collective-permute-start(f32[6,12,2,128]{3,2,1,0:T(2,128)S(1)} %get-tuple-element.86), channel_id=1, source_target_pairs={{1,0},{2,1},{3,2},{5,4},{6,5},{7,6},{9,8},{10,9},{11,10},{13,12},{... | collective-permute-start | bytes 221192 | tf_op jit(solution)/shard_map/ppermute | solution.py:20
  175.5 18.5 %copy-start.10 = (f32[8,16,128]{2,1,0:T(8,128)S(1)}, f32[8,16,128]{2,1,0:T(8,128)}, u32[]{:S(2)}) copy-start(f32[8,16,128]{2,1,0:T(8,128)} %param.22) | copy-start | bytes 196612
  175.6 19.4 %copy-start.4 = (f32[3,8,16,128]{3,2,1,0:T(8,128)}, f32[3,8,16,128]{3,2,1,0:T(8,128)S(1)}, u32[]{:S(2)}) copy-start(f32[3,8,16,128]{3,2,1,0:T(8,128)S(1)} %fusion.19) | copy-start | bytes 589828
  175.6 6.6 %collective-permute-start.12 = (f32[3,2,16,128]{3,2,1,0:T(8,128)S(1)}, f32[3,2,16,128]{3,2,1,0:T(8,128)S(1)}, u32[]{:S(2)}, u32[]{:S(2)}) collective-permute-start(f32[3,2,16,128]{3,2,1,0:T(8,128)S(1)} %get-tuple-element.117), channel_id=1, source_target_pairs={{0,4},{4,8},{8,12},{12,16},{16,20},{20,24},{24,28},{1,5},{5,9},{9,... | collective-permute-start | bytes 147464 | tf_op jit(solution)/shard_map/ppermute | solution.py:17
  180.5 6.0 %collective-permute-start.13 = (f32[3,2,16,128]{3,2,1,0:T(8,128)S(1)}, f32[3,2,16,128]{3,2,1,0:T(8,128)S(1)}, u32[]{:S(2)}, u32[]{:S(2)}) collective-permute-start(f32[3,2,16,128]{3,2,1,0:T(8,128)S(1)} %get-tuple-element.118), channel_id=1, source_target_pairs={{4,0},{8,4},{12,8},{16,12},{20,16},{24,20},{28,24},{5,1},{9,5},{13... | collective-permute-start | bytes 147464 | tf_op jit(solution)/shard_map/ppermute | solution.py:20
  186.5 5.2 %collective-permute-start.14 = (f32[3,12,2,128]{3,2,1,0:T(2,128)S(1)}, f32[3,12,2,128]{3,2,1,0:T(2,128)S(1)}, u32[]{:S(2)}, u32[]{:S(2)}) collective-permute-start(f32[3,12,2,128]{3,2,1,0:T(2,128)S(1)} %get-tuple-element.110), channel_id=1, source_target_pairs={{0,1},{1,2},{2,3},{4,5},{5,6},{6,7},{8,9},{9,10},{10,11},{12,13},{... | collective-permute-start | bytes 110600 | tf_op jit(solution)/shard_map/ppermute | solution.py:17
  190.3 3.7 %collective-permute-start.15 = (f32[3,12,2,128]{3,2,1,0:T(2,128)S(1)}, f32[3,12,2,128]{3,2,1,0:T(2,128)S(1)}, u32[]{:S(2)}, u32[]{:S(2)}) collective-permute-start(f32[3,12,2,128]{3,2,1,0:T(2,128)S(1)} %get-tuple-element.111), channel_id=1, source_target_pairs={{1,0},{2,1},{3,2},{5,4},{6,5},{7,6},{9,8},{10,9},{11,10},{13,12},{... | collective-permute-start | bytes 110600 | tf_op jit(solution)/shard_map/ppermute | solution.py:20
  (9 other events, 30.5 us)
where the time goes:
time: 200 us; the launch traced here: 197 us
  waiting for transfers between devices  79.5 us (40%)
  starting transfers between devices  60.6 us (30%)
  local copies, waits for them, and re-layouts  27.4 us (14%)
  other arithmetic  21.7 us (11%)
  matrix products  6.13 us (3%)
    all_to_all x2, waiting for transfers between devices, route_slots(): lax.all_to_all(rows, ('gx', 'gy'), split_axis=0, concat_axis=0, tiled=True)  41.5 us
    ppermute x8, starting transfers between devices, with_halo(): lax.ppermute(lax.slice_in_dim(block, block.shape[dim] - width, None, axis...  38.7 us
    ppermute x8, waiting for transfers between devices, with_halo(): lax.ppermute(lax.slice_in_dim(block, 0, width, axis=dim), axis, backward)  25.1 us
    ppermute x8, waiting for transfers between devices, with_halo(): lax.ppermute(lax.slice_in_dim(block, block.shape[dim] - width, None, axis...  12.9 us
    all_to_all x2, starting transfers between devices, route_slots(): lax.all_to_all(rows, ('gx', 'gy'), split_axis=0, concat_axis=0, tiled=True)  11.6 us
    ppermute x8, starting transfers between devices, with_halo(): lax.ppermute(lax.slice_in_dim(block, 0, width, axis=dim), axis, backward)  10.3 us
    scatter x1, local copies, waits for them, and re-layouts, shards(): jnp.zeros((slot_count, samples), jnp.bfloat16).at[slot_index]  6.71 us
    dot_general x2, matrix products, contract(): lax.dot_general(hits, rows, (((0,), (0,)), ((), ())), preferred_element_t...  6.13 us
  transfers between devices with their start and end apart: 18, of which 14 were waited for; matrix products, arithmetic and copies ran while one was open for 17% of the time, Pallas kernels for 0%

commit v1 on v0

--- a/solution.py
+++ b/solution.py
@@ -9,17 +9,15 @@
 epsilon = 1e-06
 
 
-def with_halo(block, sides, width):
-    for axis, dim in sides:
-        count = lax.axis_size(axis)
-        forward = [(i, i + 1) for i in range(count - 1)]
-        backward = [(target, source) for source, target in forward]
-        low = lax.ppermute(
-            lax.slice_in_dim(block, block.shape[dim] - width, None, axis=dim), axis, forward
-        )
-        high = lax.ppermute(lax.slice_in_dim(block, 0, width, axis=dim), axis, backward)
-        block = jnp.concatenate([low, block, high], axis=dim)
-    return block
+def halos(block, axis, dim, width=2):
+    count = lax.axis_size(axis)
+    forward = [(i, i + 1) for i in range(count - 1)]
+    backward = [(target, source) for source, target in forward]
+    low = lax.ppermute(
+        lax.slice_in_dim(block, block.shape[dim] - width, None, axis=dim), axis, forward
+    )
+    high = lax.ppermute(lax.slice_in_dim(block, 0, width, axis=dim), axis, backward)
+    return jnp.concatenate([low, block, high], axis=dim)
 
 
 def shifted(padded, start, length, axis):
@@ -38,47 +36,78 @@
     ) + far_weight * (shifted(padded, 4, length, axis) - shifted(padded, 1, length, axis))
 
 
-def pair_terms(first_rows, second_rows):
-    first_vals = first_rows.astype(jnp.float32)
-    second_vals = second_rows.astype(jnp.float32)
-    first_vals = first_vals / jnp.sqrt(
-        jnp.mean(first_vals * first_vals, axis=1, keepdims=True) + epsilon
-    )
-    second_vals = second_vals / jnp.sqrt(
-        jnp.mean(second_vals * second_vals, axis=1, keepdims=True) + epsilon
-    )
-    corr = jnp.mean(first_vals * second_vals, axis=1, keepdims=True)
-    return (
-        (second_vals - corr * first_vals).astype(jnp.bfloat16),
-        (first_vals - corr * second_vals).astype(jnp.bfloat16),
-    )
-
-
-def contract(hits, rows):
-    return lax.dot_general(hits, rows, (((0,), (0,)), ((), ())), preferred_element_type=jnp.float32)
-
-
-def route_slots(rows):
-    return lax.all_to_all(rows, ("gx", "gy"), split_axis=0, concat_axis=0, tiled=True)
+def split_halves(value):
+    top = lax.reduce_precision(value, 8, 7)
+    return top.astype(jnp.bfloat16), (value - top).astype(jnp.bfloat16)
+
+
+def partner_sums(scaled, station_pairs, devices):
+    stations = scaled.shape[0]
+    pairs = station_pairs.shape[0]
+    if stations > 1024:
+        first, second = station_pairs[:, 0], station_pairs[:, 1]
+        total = jnp.zeros_like(scaled).at[first].add(scaled[second])
+        return total.at[second].add(scaled[first])
+    held = stations // devices
+    blocks = station_pairs.reshape(devices, pairs // devices, 2)
+    offset = jnp.arange(devices)[:, None] * held
+    first_hot = ((blocks[:, :, 0] - offset)[:, :, None] == jnp.arange(held)).astype(jnp.bfloat16)
+    second_hot = (blocks[:, :, 1][:, :, None] == jnp.arange(stations)).astype(jnp.bfloat16)
+    counts = (
+        jnp.einsum("bpj,bpt->bjt", first_hot, second_hot, preferred_element_type=jnp.float32)
+        .astype(jnp.bfloat16)
+        .reshape(stations, stations)
+    )
+    both = jnp.concatenate(split_halves(scaled), axis=1)
+    width = scaled.shape[1]
+    total = lax.dot_general(
+        counts, both, (((1,), (0,)), ((), ())), preferred_element_type=jnp.float32
+    ) + lax.dot_general(
+        counts, both, (((0,), (0,)), ((), ())), preferred_element_type=jnp.float32
+    )
+    return total[:, :width] + total[:, width:]
+
+
+def adjoint_rows(residuals, station_pairs):
+    axes = ("gx", "gy")
+    held, samples = residuals.shape
+    devices = lax.axis_size(axes)
+    chunk = samples // devices
+    values = residuals.astype(jnp.float32)
+    inverse = 1.0 / jnp.sqrt(jnp.mean(values * values, axis=1, keepdims=True) + epsilon)
+    inverse_top, inverse_rest = split_halves(inverse.reshape(1, held))
+    scales = jnp.concatenate([inverse_top, inverse_rest], axis=0)
+    scales = jnp.pad(scales, ((0, 14), (0, chunk - held)))
+    payload = jnp.concatenate(
+        [
+            residuals.reshape(held, devices, chunk).transpose(1, 0, 2),
+            jnp.broadcast_to(scales[None], (devices, 16, chunk)),
+        ],
+        axis=1,
+    )
+    arrived = lax.all_to_all(payload, axes, split_axis=0, concat_axis=0, tiled=True)
+    arrived_scales = arrived[:, held, :held].astype(jnp.float32) + arrived[
+        :, held + 1, :held
+    ].astype(jnp.float32)
+    scaled = (arrived[:, :held].astype(jnp.float32) * arrived_scales[:, :, None]).reshape(
+        devices * held, chunk
+    )
+    sums = partner_sums(scaled, station_pairs, devices).reshape(devices, held, chunk)
+    back = lax.all_to_all(sums, axes, split_axis=0, concat_axis=0, tiled=True)
+    back = back.transpose(1, 0, 2).reshape(held, samples)
+    normed = values * inverse
+    corr_sum = jnp.mean(normed * back, axis=1, keepdims=True)
+    return back - corr_sum * normed
 
 
 def stress_sides(stress):
-    cells_first = stress.shape[1]
-    cells_second = stress.shape[2]
-    wide_stress = with_halo(stress, (("gx", 1), ("gy", 2)), 2)
-    first_part = wide_stress[:, :, 2 : 2 + cells_second, :]
-    second_part = wide_stress[:, 2 : 2 + cells_first, :, :]
-    return (
-        (first_part[0], first_part[3], first_part[4]),
-        (second_part[1], second_part[3], second_part[5]),
-    )
+    first = halos(jnp.stack([stress[0], stress[3], stress[4]]), "gx", 1)
+    second = halos(jnp.stack([stress[1], stress[3], stress[5]]), "gy", 2)
+    return (first, second)
 
 
 def motion_sides(moved):
-    cells_first = moved.shape[1]
-    cells_second = moved.shape[2]
-    wide_motion = with_halo(moved, (("gx", 1), ("gy", 2)), 2)
-    return (wide_motion[:, :, 2 : 2 + cells_second, :], wide_motion[:, 2 : 2 + cells_first, :, :])
+    return (halos(moved, "gx", 1), halos(moved, "gy", 2))
 
 
 def advance(
@@ -169,43 +198,8 @@
     station_cell,
     station_pairs,
 ):
-    stations_here = residuals.shape[0]
     samples = residuals.shape[1]
-    devices = lax.axis_size(("gx", "gy"))
-    pair_rows = station_pairs.shape[0] // devices
-    slot_count = 2 * pair_rows
-    capacity = slot_count // devices
-    device_index = lax.axis_index(("gx", "gy"))
-    own_pairs = lax.dynamic_slice_in_dim(station_pairs, device_index * pair_rows, pair_rows, 0)
-    first_local = own_pairs[:, 0] - device_index * stations_here
-    owner_device = own_pairs[:, 1] // stations_here
-    order_index = jnp.arange(pair_rows)
-    earlier = (owner_device[:, None] == owner_device[None, :]) & (
-        order_index[None, :] < order_index[:, None]
-    )
-    slot_index = owner_device * capacity + jnp.sum(earlier.astype(jnp.int32), axis=1)
-    blocks = station_pairs.reshape(devices, pair_rows, 2)
-    mine_mask = (blocks[:, :, 1] // stations_here == device_index).astype(jnp.int32)
-    before = jnp.cumsum(mine_mask, axis=1) - mine_mask
-    matches = (
-        (mine_mask[:, :, None] > 0) & (before[:, :, None] == jnp.arange(capacity)[None, None, :])
-    ).astype(jnp.int32)
-    wanted = (blocks[:, :, 1] % stations_here)[:, :, None]
-    found = jnp.sum(matches, axis=1)
-    picked = jnp.sum(matches * wanted, axis=1)
-    asked_ids = jnp.where(found > 0, picked, -1).reshape(slot_count)
-    station_ids = jnp.arange(stations_here)
-    first_hits = (first_local[:, None] == station_ids[None, :]).astype(jnp.bfloat16)
-    asked_hits = (asked_ids[:, None] == station_ids[None, :]).astype(jnp.bfloat16)
-    first_rows = residuals[first_local]
-    local_rows = jnp.where(
-        asked_ids[:, None] >= 0, residuals[jnp.maximum(asked_ids, 0)], jnp.zeros((), jnp.bfloat16)
-    )
-    carried = jnp.zeros((slot_count, samples), jnp.bfloat16).at[slot_index].set(first_rows)
-    arrived = route_slots(carried)
-    toward_first, toward_second = pair_terms(arrived, local_rows)
-    returned = route_slots(toward_first)
-    adjoint = contract(first_hits, returned[slot_index]) + contract(asked_hits, toward_second)
+    adjoint = adjoint_rows(residuals, station_pairs)
     cells_first = velocity.shape[1]
     cells_second = velocity.shape[2]
     step_count = forward_strain.shape[0] // 6

time: 200 us -> 105 us (0.53)
  the two profiles are of different devices: /device:TPU:0 before, /device:TPU:6 now
where the time goes in v1:
time: 105 us
  starting transfers between devices  59.6 us (57%)
  waiting for transfers between devices  23.8 us (23%)
  matrix products  7.75 us (7%)
  other arithmetic  7.3 us (7%)
  local copies, waits for them, and re-layouts  4.58 us (4%)
  between operations  1.63 us (2%)
    ppermute x8, starting transfers between devices, halos(): lax.ppermute(lax.slice_in_dim(block, 0, width, axis=dim), axis, backward)  24.6 us
    ppermute x8, starting transfers between devices, halos(): lax.ppermute(lax.slice_in_dim(block, block.shape[dim] - width, None, axis...  24.1 us
    all_to_all x1, waiting for transfers between devices, adjoint_rows(): back = lax.all_to_all(sums, axes, split_axis=0, concat_axis=0, tiled=True)  14.2 us
    ppermute x8, waiting for transfers between devices, halos(): lax.ppermute(lax.slice_in_dim(block, 0, width, axis=dim), axis, backward)  7.98 us
    all_to_all x1, starting transfers between devices, adjoint_rows(): lax.all_to_all(payload, axes, split_axis=0, concat_axis=0, tiled=True)  6.07 us
    all_to_all x1, starting transfers between devices, adjoint_rows(): back = lax.all_to_all(sums, axes, split_axis=0, concat_axis=0, tiled=True)  4.87 us
    dot_general x1, matrix products, partner_sums(): jnp.einsum('bpj,bpt->bjt', first_hot, second_hot, preferred_element_type=...  4.54 us
    dot_general x1, matrix products, partner_sums(): lax.dot_general(counts, both, (((1,), (0,)), ((), ())), preferred_element...  2.46 us
  transfers between devices with their start and end apart: 18, of which 4 were waited for; matrix products, arithmetic and copies ran while one was open for 10% of the time, Pallas kernels for 0%

profile of v1, /device:TPU:6, one launch (start us, length us, event | category | flops | bytes accessed | tf_op | source)
XLA Modules:
  0.0 104.6 jit_solution(17648827908925660126)
XLA Ops:
  3.9 6.1 %all-to-all-start = ((bf16[32,48,128]{2,1,0:T(8,128)(2,1)}), bf16[32,48,128]{2,1,0:T(8,128)(2,1)S(1)}, u32[]{:S(2)}, u32[]{:S(2)}) async-start(bf16[32,48,128]{2,1,0:T(8,128)(2,1)} %copy.378), calls=%async_computation | async-start | bytes 786432 | tf_op jit(solution)/shard_map/all_to_all | solution.py:88
  10.0 2.1 %collective-permute-start.2 = (f32[3,8,2,128]{3,1,2,0:T(8,128)S(1)}, f32[3,8,2,128]{3,1,2,0:T(8,128)S(1)}, u32[]{:S(2)}, u32[]{:S(2)}) collective-permute-start(f32[3,8,2,128]{3,1,2,0:T(8,128)S(1)} %copy.374), channel_id=1, source_target_pairs={{0,1},{1,2},{2,3},{4,5},{5,6},{6,7},{8,9},{9,10},{10,11},{12,13},{... | collective-permute-start | bytes 73736 | tf_op jit(solution)/shard_map/ppermute | solution.py:16
  12.1 3.5 %collective-permute-start.3 = (f32[3,8,2,128]{3,1,2,0:T(8,128)S(1)}, f32[3,8,2,128]{3,1,2,0:T(8,128)S(1)}, u32[]{:S(2)}, u32[]{:S(2)}) collective-permute-start(f32[3,8,2,128]{3,1,2,0:T(8,128)S(1)} %copy.375), channel_id=1, source_target_pairs={{1,0},{2,1},{3,2},{5,4},{6,5},{7,6},{9,8},{10,9},{11,10},{13,12},{... | collective-permute-start | bytes 73736 | tf_op jit(solution)/shard_map/ppermute | solution.py:19
  15.6 2.5 %collective-permute-start = (f32[3,2,16,128]{3,2,1,0:T(8,128)S(1)}, f32[3,2,16,128]{3,2,1,0:T(8,128)S(1)}, u32[]{:S(2)}, u32[]{:S(2)}) collective-permute-start(f32[3,2,16,128]{3,2,1,0:T(8,128)S(1)} %get-tuple-element.132), channel_id=1, source_target_pairs={{4,0},{8,4},{12,8},{16,12},{20,16},{24,20},{28,24},{5,1},{9,5},{13... | collective-permute-start | bytes 147464 | tf_op jit(solution)/shard_map/ppermute | solution.py:19
  18.1 4.3 %collective-permute-start.1 = (f32[3,2,16,128]{3,2,1,0:T(8,128)S(1)}, f32[3,2,16,128]{3,2,1,0:T(8,128)S(1)}, u32[]{:S(2)}, u32[]{:S(2)}) collective-permute-start(f32[3,2,16,128]{3,2,1,0:T(8,128)S(1)} %get-tuple-element.133), channel_id=1, source_target_pairs={{0,4},{4,8},{8,12},{12,16},{16,20},{20,24},{24,28},{1,5},{5,9},{9,... | collective-permute-start | bytes 147464 | tf_op jit(solution)/shard_map/ppermute | solution.py:16
  22.6 4.5 %fusion.2 = bf16[32,32,1024]{2,1,0:T(8,128)(2,1)} fusion(s32[32,128]{1,0:T(8,128)S(1)} %get-tuple-element.137, s32[32,128]{1,0:T(8,128)S(1)} %get-tuple-element.136), kind=kOutput, calls=%fused_computation.3 | convolution fusion | flops 273809408 | bytes 2129920 | tf_op jit(solution)/shard_map/bpj,bpt->bjt/dot_general | solution.py:57
  27.8 2.5 %fusion.9 = f32[1024,256]{1,0:T(8,128)S(1)} fusion(bf16[1024,1024]{1,0:T(8,128)(2,1)} %bitcast.267, bf16[1024,128]{1,0:T(8,128)(2,1)S(1)} %get-tuple-element.81, bf16[1024,128]{1,0:T(8,128)(2,1)S(1)} %get-tuple-element.80), kind=kOutput, calls=%fused_computation.48 | convolution fusion | flops 537919488 | bytes 3670016 | tf_op jit(solution)/shard_map/dot_general | solution.py:63
  31.9 4.9 %all-to-all-start.1 = ((f32[32,32,128]{2,1,0:T(8,128)}), f32[32,32,128]{2,1,0:T(8,128)S(1)}, u32[]{:S(2)}, u32[]{:S(2)}) async-start(f32[32,32,128]{2,1,0:T(8,128)} %bitcast.19), calls=%async_computation.1 | async-start | bytes 1048576 | tf_op jit(solution)/shard_map/all_to_all | solution.py:96
  37.3 14.2 %all-to-all-done.1 = f32[32,32,128]{2,1,0:T(8,128)S(1)} async-done(((f32[32,32,128]{2,1,0:T(8,128)}), f32[32,32,128]{2,1,0:T(8,128)S(1)}, u32[]{:S(2)}, u32[]{:S(2)}) %all-to-all-start.1) | async-done | bytes 524320 | tf_op jit(solution)/shard_map/all_to_all | solution.py:96
  53.4 1.9 %collective-permute-start.6 = (f32[3,8,2,128]{3,1,2,0:T(8,128)S(1)}, f32[3,8,2,128]{3,1,2,0:T(8,128)S(1)}, u32[]{:S(2)}, u32[]{:S(2)}) collective-permute-start(f32[3,8,2,128]{3,1,2,0:T(8,128)S(1)} %copy.382), channel_id=1, source_target_pairs={{0,1},{1,2},{2,3},{4,5},{5,6},{6,7},{8,9},{9,10},{10,11},{12,13},{... | collective-permute-start | bytes 73736 | tf_op jit(solution)/shard_map/ppermute | solution.py:16
  55.4 3.6 %collective-permute-start.7 = (f32[3,8,2,128]{3,1,2,0:T(8,128)S(1)}, f32[3,8,2,128]{3,1,2,0:T(8,128)S(1)}, u32[]{:S(2)}, u32[]{:S(2)}) collective-permute-start(f32[3,8,2,128]{3,1,2,0:T(8,128)S(1)} %copy.383), channel_id=1, source_target_pairs={{1,0},{2,1},{3,2},{5,4},{6,5},{7,6},{9,8},{10,9},{11,10},{13,12},{... | collective-permute-start | bytes 73736 | tf_op jit(solution)/shard_map/ppermute | solution.py:19
  59.2 2.5 %collective-permute-start.4 = (f32[3,2,16,128]{3,2,1,0:T(8,128)S(1)}, f32[3,2,16,128]{3,2,1,0:T(8,128)S(1)}, u32[]{:S(2)}, u32[]{:S(2)}) collective-permute-start(f32[3,2,16,128]{3,2,1,0:T(8,128)S(1)} %get-tuple-element.126), channel_id=1, source_target_pairs={{0,4},{4,8},{8,12},{12,16},{16,20},{20,24},{24,28},{1,5},{5,9},{9,... | collective-permute-start | bytes 147464 | tf_op jit(solution)/shard_map/ppermute | solution.py:16
  61.7 3.3 %collective-permute-start.5 = (f32[3,2,16,128]{3,2,1,0:T(8,128)S(1)}, f32[3,2,16,128]{3,2,1,0:T(8,128)S(1)}, u32[]{:S(2)}, u32[]{:S(2)}) collective-permute-start(f32[3,2,16,128]{3,2,1,0:T(8,128)S(1)} %get-tuple-element.127), channel_id=1, source_target_pairs={{4,0},{8,4},{12,8},{16,12},{20,16},{24,20},{28,24},{5,1},{9,5},{13... | collective-permute-start | bytes 147464 | tf_op jit(solution)/shard_map/ppermute | solution.py:19
  65.4 3.2 %collective-permute-done.5 = f32[3,2,16,128]{3,2,1,0:T(8,128)S(1)} collective-permute-done((f32[3,2,16,128]{3,2,1,0:T(8,128)S(1)}, f32[3,2,16,128]{3,2,1,0:T(8,128)S(1)}, u32[]{:S(2)}, u32[]{:S(2)}) %collective-permute-start.5) | collective-permute-done | bytes 49184 | tf_op jit(solution)/shard_map/ppermute | solution.py:19
  69.4 1.9 %collective-permute-start.10 = (f32[3,8,2,128]{3,1,2,0:T(8,128)S(1)}, f32[3,8,2,128]{3,1,2,0:T(8,128)S(1)}, u32[]{:S(2)}, u32[]{:S(2)}) collective-permute-start(f32[3,8,2,128]{3,1,2,0:T(8,128)S(1)} %copy.386), channel_id=1, source_target_pairs={{0,1},{1,2},{2,3},{4,5},{5,6},{6,7},{8,9},{9,10},{10,11},{12,13},{... | collective-permute-start | bytes 73736 | tf_op jit(solution)/shard_map/ppermute | solution.py:16
  71.4 3.6 %collective-permute-start.11 = (f32[3,8,2,128]{3,1,2,0:T(8,128)S(1)}, f32[3,8,2,128]{3,1,2,0:T(8,128)S(1)}, u32[]{:S(2)}, u32[]{:S(2)}) collective-permute-start(f32[3,8,2,128]{3,1,2,0:T(8,128)S(1)} %copy.387), channel_id=1, source_target_pairs={{1,0},{2,1},{3,2},{5,4},{6,5},{7,6},{9,8},{10,9},{11,10},{13,12},{... | collective-permute-start | bytes 73736 | tf_op jit(solution)/shard_map/ppermute | solution.py:19
  75.0 2.4 %collective-permute-start.8 = (f32[3,2,16,128]{3,2,1,0:T(8,128)S(1)}, f32[3,2,16,128]{3,2,1,0:T(8,128)S(1)}, u32[]{:S(2)}, u32[]{:S(2)}) collective-permute-start(f32[3,2,16,128]{3,2,1,0:T(8,128)S(1)} %get-tuple-element.119), channel_id=1, source_target_pairs={{4,0},{8,4},{12,8},{16,12},{20,16},{24,20},{28,24},{5,1},{9,5},{13... | collective-permute-start | bytes 147464 | tf_op jit(solution)/shard_map/ppermute | solution.py:19
  77.5 4.3 %collective-permute-start.9 = (f32[3,2,16,128]{3,2,1,0:T(8,128)S(1)}, f32[3,2,16,128]{3,2,1,0:T(8,128)S(1)}, u32[]{:S(2)}, u32[]{:S(2)}) collective-permute-start(f32[3,2,16,128]{3,2,1,0:T(8,128)S(1)} %get-tuple-element.120), channel_id=1, source_target_pairs={{0,4},{4,8},{8,12},{12,16},{16,20},{20,24},{24,28},{1,5},{5,9},{9,... | collective-permute-start | bytes 147464 | tf_op jit(solution)/shard_map/ppermute | solution.py:16
  82.0 1.6 %collective-permute-done.9 = f32[3,2,16,128]{3,2,1,0:T(8,128)S(1)} collective-permute-done((f32[3,2,16,128]{3,2,1,0:T(8,128)S(1)}, f32[3,2,16,128]{3,2,1,0:T(8,128)S(1)}, u32[]{:S(2)}, u32[]{:S(2)}) %collective-permute-start.9) | collective-permute-done | bytes 49184 | tf_op jit(solution)/shard_map/ppermute | solution.py:16
  84.2 1.9 %collective-permute-start.14 = (f32[3,8,2,128]{3,1,2,0:T(8,128)S(1)}, f32[3,8,2,128]{3,1,2,0:T(8,128)S(1)}, u32[]{:S(2)}, u32[]{:S(2)}) collective-permute-start(f32[3,8,2,128]{3,1,2,0:T(8,128)S(1)} %copy.392), channel_id=1, source_target_pairs={{0,1},{1,2},{2,3},{4,5},{5,6},{6,7},{8,9},{9,10},{10,11},{12,13},{... | collective-permute-start | bytes 73736 | tf_op jit(solution)/shard_map/ppermute | solution.py:16
  86.2 3.6 %collective-permute-start.15 = (f32[3,8,2,128]{3,1,2,0:T(8,128)S(1)}, f32[3,8,2,128]{3,1,2,0:T(8,128)S(1)}, u32[]{:S(2)}, u32[]{:S(2)}) collective-permute-start(f32[3,8,2,128]{3,1,2,0:T(8,128)S(1)} %copy.393), channel_id=1, source_target_pairs={{1,0},{2,1},{3,2},{5,4},{6,5},{7,6},{9,8},{10,9},{11,10},{13,12},{... | collective-permute-start | bytes 73736 | tf_op jit(solution)/shard_map/ppermute | solution.py:19
  90.0 5.1 %collective-permute-start.12 = (f32[3,2,16,128]{3,2,1,0:T(8,128)S(1)}, f32[3,2,16,128]{3,2,1,0:T(8,128)S(1)}, u32[]{:S(2)}, u32[]{:S(2)}) collective-permute-start(f32[3,2,16,128]{3,2,1,0:T(8,128)S(1)} %get-tuple-element.114), channel_id=1, source_target_pairs={{0,4},{4,8},{8,12},{12,16},{16,20},{20,24},{24,28},{1,5},{5,9},{9,... | collective-permute-start | bytes 147464 | tf_op jit(solution)/shard_map/ppermute | solution.py:16
  95.2 1.9 %collective-permute-start.13 = (f32[3,2,16,128]{3,2,1,0:T(8,128)S(1)}, f32[3,2,16,128]{3,2,1,0:T(8,128)S(1)}, u32[]{:S(2)}, u32[]{:S(2)}) collective-permute-start(f32[3,2,16,128]{3,2,1,0:T(8,128)S(1)} %get-tuple-element.113), channel_id=1, source_target_pairs={{4,0},{8,4},{12,8},{16,12},{20,16},{24,20},{28,24},{5,1},{9,5},{13... | collective-permute-start | bytes 147464 | tf_op jit(solution)/shard_map/ppermute | solution.py:19
  97.3 4.8 %collective-permute-done.13 = f32[3,2,16,128]{3,2,1,0:T(8,128)S(1)} collective-permute-done((f32[3,2,16,128]{3,2,1,0:T(8,128)S(1)}, f32[3,2,16,128]{3,2,1,0:T(8,128)S(1)}, u32[]{:S(2)}, u32[]{:S(2)}) %collective-permute-start.13) | collective-permute-done | bytes 49184 | tf_op jit(solution)/shard_map/ppermute | solution.py:19
  (139 shorter events, 12.7 us)
Async XLA Ops:
  2.8 19.6 %copy-start.12 = (s32[4096,2]{0,1:T(2,128)S(1)}, s32[4096,2]{0,1:T(2,128)}, u32[]{:S(2)}) copy-start(s32[4096,2]{0,1:T(2,128)} %param.25) | copy-start | bytes 98308
  2.8 19.6 %copy-start.11 = (f32[8,16,128]{2,1,0:T(8,128)S(1)}, f32[8,16,128]{2,1,0:T(8,128)}, u32[]{:S(2)}) copy-start(f32[8,16,128]{2,1,0:T(8,128)} %param.19) | copy-start | bytes 196612
  2.9 19.7 %copy-start.6 = (bf16[12,8,16,128]{3,2,1,0:T(8,128)(2,1)S(1)}, bf16[12,8,16,128]{3,2,1,0:T(8,128)(2,1)}, u32[]{:S(2)}) copy-start(bf16[12,8,16,128]{3,2,1,0:T(8,128)(2,1)} %param.20) | copy-start | bytes 1179652
  3.9 23.6 %all-to-all-start = ((bf16[32,48,128]{2,1,0:T(8,128)(2,1)}), bf16[32,48,128]{2,1,0:T(8,128)(2,1)S(1)}, u32[]{:S(2)}, u32[]{:S(2)}) async-start(bf16[32,48,128]{2,1,0:T(8,128)(2,1)} %copy.378), calls=%async_computation | async-start | bytes 786432 | tf_op jit(solution)/shard_map/all_to_all | solution.py:88
  10.0 17.3 %collective-permute-start.2 = (f32[3,8,2,128]{3,1,2,0:T(8,128)S(1)}, f32[3,8,2,128]{3,1,2,0:T(8,128)S(1)}, u32[]{:S(2)}, u32[]{:S(2)}) collective-permute-start(f32[3,8,2,128]{3,1,2,0:T(8,128)S(1)} %copy.374), channel_id=1, source_target_pairs={{0,1},{1,2},{2,3},{4,5},{5,6},{6,7},{8,9},{9,10},{10,11},{12,13},{... | collective-permute-start | bytes 73736 | tf_op jit(solution)/shard_map/ppermute | solution.py:16
  12.1 15.3 %collective-permute-start.3 = (f32[3,8,2,128]{3,1,2,0:T(8,128)S(1)}, f32[3,8,2,128]{3,1,2,0:T(8,128)S(1)}, u32[]{:S(2)}, u32[]{:S(2)}) collective-permute-start(f32[3,8,2,128]{3,1,2,0:T(8,128)S(1)} %copy.375), channel_id=1, source_target_pairs={{1,0},{2,1},{3,2},{5,4},{6,5},{7,6},{9,8},{10,9},{11,10},{13,12},{... | collective-permute-start | bytes 73736 | tf_op jit(solution)/shard_map/ppermute | solution.py:19
  15.6 21.1 %collective-permute-start = (f32[3,2,16,128]{3,2,1,0:T(8,128)S(1)}, f32[3,2,16,128]{3,2,1,0:T(8,128)S(1)}, u32[]{:S(2)}, u32[]{:S(2)}) collective-permute-start(f32[3,2,16,128]{3,2,1,0:T(8,128)S(1)} %get-tuple-element.132), channel_id=1, source_target_pairs={{4,0},{8,4},{12,8},{16,12},{20,16},{24,20},{28,24},{5,1},{9,5},{13... | collective-permute-start | bytes 147464 | tf_op jit(solution)/shard_map/ppermute | solution.py:19
  18.1 18.7 %collective-permute-start.1 = (f32[3,2,16,128]{3,2,1,0:T(8,128)S(1)}, f32[3,2,16,128]{3,2,1,0:T(8,128)S(1)}, u32[]{:S(2)}, u32[]{:S(2)}) collective-permute-start(f32[3,2,16,128]{3,2,1,0:T(8,128)S(1)} %get-tuple-element.133), channel_id=1, source_target_pairs={{0,4},{4,8},{8,12},{12,16},{16,20},{20,24},{24,28},{1,5},{5,9},{9,... | collective-permute-start | bytes 147464 | tf_op jit(solution)/shard_map/ppermute | solution.py:16
  31.9 19.6 %all-to-all-start.1 = ((f32[32,32,128]{2,1,0:T(8,128)}), f32[32,32,128]{2,1,0:T(8,128)S(1)}, u32[]{:S(2)}, u32[]{:S(2)}) async-start(f32[32,32,128]{2,1,0:T(8,128)} %bitcast.19), calls=%async_computation.1 | async-start | bytes 1048576 | tf_op jit(solution)/shard_map/all_to_all | solution.py:96
  51.7 16.9 %copy-start = (f32[8,16,128]{2,1,0:T(8,128)S(1)}, f32[8,16,128]{2,1,0:T(8,128)}, u32[]{:S(2)}) copy-start(f32[8,16,128]{2,1,0:T(8,128)} %param.18) | copy-start | bytes 196612
  53.4 11.8 %collective-permute-start.6 = (f32[3,8,2,128]{3,1,2,0:T(8,128)S(1)}, f32[3,8,2,128]{3,1,2,0:T(8,128)S(1)}, u32[]{:S(2)}, u32[]{:S(2)}) collective-permute-start(f32[3,8,2,128]{3,1,2,0:T(8,128)S(1)} %copy.382), channel_id=1, source_target_pairs={{0,1},{1,2},{2,3},{4,5},{5,6},{6,7},{8,9},{9,10},{10,11},{12,13},{... | collective-permute-start | bytes 73736 | tf_op jit(solution)/shard_map/ppermute | solution.py:16
  55.4 9.9 %collective-permute-start.7 = (f32[3,8,2,128]{3,1,2,0:T(8,128)S(1)}, f32[3,8,2,128]{3,1,2,0:T(8,128)S(1)}, u32[]{:S(2)}, u32[]{:S(2)}) collective-permute-start(f32[3,8,2,128]{3,1,2,0:T(8,128)S(1)} %copy.383), channel_id=1, source_target_pairs={{1,0},{2,1},{3,2},{5,4},{6,5},{7,6},{9,8},{10,9},{11,10},{13,12},{... | collective-permute-start | bytes 73736 | tf_op jit(solution)/shard_map/ppermute | solution.py:19
  59.2 6.2 %collective-permute-start.4 = (f32[3,2,16,128]{3,2,1,0:T(8,128)S(1)}, f32[3,2,16,128]{3,2,1,0:T(8,128)S(1)}, u32[]{:S(2)}, u32[]{:S(2)}) collective-permute-start(f32[3,2,16,128]{3,2,1,0:T(8,128)S(1)} %get-tuple-element.126), channel_id=1, source_target_pairs={{0,4},{4,8},{8,12},{12,16},{16,20},{20,24},{24,28},{1,5},{5,9},{9,... | collective-permute-start | bytes 147464 | tf_op jit(solution)/shard_map/ppermute | solution.py:16
  61.7 6.9 %collective-permute-start.5 = (f32[3,2,16,128]{3,2,1,0:T(8,128)S(1)}, f32[3,2,16,128]{3,2,1,0:T(8,128)S(1)}, u32[]{:S(2)}, u32[]{:S(2)}) collective-permute-start(f32[3,2,16,128]{3,2,1,0:T(8,128)S(1)} %get-tuple-element.127), channel_id=1, source_target_pairs={{4,0},{8,4},{12,8},{16,12},{20,16},{24,20},{28,24},{5,1},{9,5},{13... | collective-permute-start | bytes 147464 | tf_op jit(solution)/shard_map/ppermute | solution.py:19
  69.4 12.4 %collective-permute-start.10 = (f32[3,8,2,128]{3,1,2,0:T(8,128)S(1)}, f32[3,8,2,128]{3,1,2,0:T(8,128)S(1)}, u32[]{:S(2)}, u32[]{:S(2)}) collective-permute-start(f32[3,8,2,128]{3,1,2,0:T(8,128)S(1)} %copy.386), channel_id=1, source_target_pairs={{0,1},{1,2},{2,3},{4,5},{5,6},{6,7},{8,9},{9,10},{10,11},{12,13},{... | collective-permute-start | bytes 73736 | tf_op jit(solution)/shard_map/ppermute | solution.py:16
  71.4 10.5 %collective-permute-start.11 = (f32[3,8,2,128]{3,1,2,0:T(8,128)S(1)}, f32[3,8,2,128]{3,1,2,0:T(8,128)S(1)}, u32[]{:S(2)}, u32[]{:S(2)}) collective-permute-start(f32[3,8,2,128]{3,1,2,0:T(8,128)S(1)} %copy.387), channel_id=1, source_target_pairs={{1,0},{2,1},{3,2},{5,4},{6,5},{7,6},{9,8},{10,9},{11,10},{13,12},{... | collective-permute-start | bytes 73736 | tf_op jit(solution)/shard_map/ppermute | solution.py:19
  75.0 6.9 %collective-permute-start.8 = (f32[3,2,16,128]{3,2,1,0:T(8,128)S(1)}, f32[3,2,16,128]{3,2,1,0:T(8,128)S(1)}, u32[]{:S(2)}, u32[]{:S(2)}) collective-permute-start(f32[3,2,16,128]{3,2,1,0:T(8,128)S(1)} %get-tuple-element.119), channel_id=1, source_target_pairs={{4,0},{8,4},{12,8},{16,12},{20,16},{24,20},{28,24},{5,1},{9,5},{13... | collective-permute-start | bytes 147464 | tf_op jit(solution)/shard_map/ppermute | solution.py:19
  77.5 6.1 %collective-permute-start.9 = (f32[3,2,16,128]{3,2,1,0:T(8,128)S(1)}, f32[3,2,16,128]{3,2,1,0:T(8,128)S(1)}, u32[]{:S(2)}, u32[]{:S(2)}) collective-permute-start(f32[3,2,16,128]{3,2,1,0:T(8,128)S(1)} %get-tuple-element.120), channel_id=1, source_target_pairs={{0,4},{4,8},{8,12},{12,16},{16,20},{20,24},{24,28},{1,5},{5,9},{9,... | collective-permute-start | bytes 147464 | tf_op jit(solution)/shard_map/ppermute | solution.py:16
  83.8 18.2 %copy-start.9 = (f32[8,16,128]{2,1,0:T(8,128)S(1)}, f32[8,16,128]{2,1,0:T(8,128)}, u32[]{:S(2)}) copy-start(f32[8,16,128]{2,1,0:T(8,128)} %param.22) | copy-start | bytes 196612
  84.2 18.8 %copy-start.1 = (f32[3,8,16,128]{3,2,1,0:T(8,128)}, f32[3,8,16,128]{3,2,1,0:T(8,128)S(1)}, u32[]{:S(2)}) copy-start(f32[3,8,16,128]{3,2,1,0:T(8,128)S(1)} %fusion.12) | copy-start | bytes 589828
  84.2 12.8 %collective-permute-start.14 = (f32[3,8,2,128]{3,1,2,0:T(8,128)S(1)}, f32[3,8,2,128]{3,1,2,0:T(8,128)S(1)}, u32[]{:S(2)}, u32[]{:S(2)}) collective-permute-start(f32[3,8,2,128]{3,1,2,0:T(8,128)S(1)} %copy.392), channel_id=1, source_target_pairs={{0,1},{1,2},{2,3},{4,5},{5,6},{6,7},{8,9},{9,10},{10,11},{12,13},{... | collective-permute-start | bytes 73736 | tf_op jit(solution)/shard_map/ppermute | solution.py:16
  86.2 10.9 %collective-permute-start.15 = (f32[3,8,2,128]{3,1,2,0:T(8,128)S(1)}, f32[3,8,2,128]{3,1,2,0:T(8,128)S(1)}, u32[]{:S(2)}, u32[]{:S(2)}) collective-permute-start(f32[3,8,2,128]{3,1,2,0:T(8,128)S(1)} %copy.393), channel_id=1, source_target_pairs={{1,0},{2,1},{3,2},{5,4},{6,5},{7,6},{9,8},{10,9},{11,10},{13,12},{... | collective-permute-start | bytes 73736 | tf_op jit(solution)/shard_map/ppermute | solution.py:19
  90.0 7.2 %collective-permute-start.12 = (f32[3,2,16,128]{3,2,1,0:T(8,128)S(1)}, f32[3,2,16,128]{3,2,1,0:T(8,128)S(1)}, u32[]{:S(2)}, u32[]{:S(2)}) collective-permute-start(f32[3,2,16,128]{3,2,1,0:T(8,128)S(1)} %get-tuple-element.114), channel_id=1, source_target_pairs={{0,4},{4,8},{8,12},{12,16},{16,20},{20,24},{24,28},{1,5},{5,9},{9,... | collective-permute-start | bytes 147464 | tf_op jit(solution)/shard_map/ppermute | solution.py:16
  95.2 6.9 %collective-permute-start.13 = (f32[3,2,16,128]{3,2,1,0:T(8,128)S(1)}, f32[3,2,16,128]{3,2,1,0:T(8,128)S(1)}, u32[]{:S(2)}, u32[]{:S(2)}) collective-permute-start(f32[3,2,16,128]{3,2,1,0:T(8,128)S(1)} %get-tuple-element.113), channel_id=1, source_target_pairs={{4,0},{8,4},{12,8},{16,12},{20,16},{24,20},{28,24},{5,1},{9,5},{13... | collective-permute-start | bytes 147464 | tf_op jit(solution)/shard_map/ppermute | solution.py:19
  (9 other events, 83.1 us)

commit v2 on v1

v2 whole, which is shorter than its diff:
```python
import functools

import jax
import jax.numpy as jnp
from jax import lax
from jax.experimental import pallas as pl
from jax.experimental.pallas import tpu as pltpu
from jax.sharding import PartitionSpec as P

near_weight = 9.0 / 8.0
far_weight = -1.0 / 24.0
time_step = 0.25
epsilon = 1e-06


def shift_third(field, shift):
    cells = field.shape[2]
    position = lax.broadcasted_iota(jnp.int32, field.shape, 2) + shift
    moved = pltpu.roll(field, (-shift) % cells, 2)
    return jnp.where((position >= 0) & (position < cells), moved, 0.0)


def combine(at_two, at_one, at_three, at_zero):
    return near_weight * (at_two - at_one) + far_weight * (at_three - at_zero)


def third_back(field):
    return combine(field, shift_third(field, -1), shift_third(field, 1), shift_third(field, -2))


def third_ahead(field):
    return combine(shift_third(field, 1), field, shift_third(field, 2), shift_third(field, -1))


def stencil_kernel(
    counts,
    velocity,
    stress,
    lame_first,
    shear_modulus,
    buoyancy,
    strain,
    lame_accum,
    shear_accum,
    surface,
    velocity_out,
    stress_out,
    lame_out,
    shear_out,
    wide_x,
    wide_y,
    send_sem,
    recv_sem,
):
    steps = surface.shape[0]
    cells_x, cells_y = velocity.shape[1], velocity.shape[2]
    place = (lax.axis_index("gx"), lax.axis_index("gy"))

    def neighbour(axis, step):
        target = list(place)
        target[axis] = place[axis] + step
        return tuple(target)

    def present(axis, step):
        return place[axis] < counts[axis] - 1 if step > 0 else place[axis] > 0

    sides = ((0, 1), (0, -1), (1, 1), (1, -1))
    for axis, step in sides:

        @pl.when(jnp.logical_not(present(axis, step)))
        def _():
            for phase in range(2 * steps):
                if axis == 0:
                    low = cells_x + 2 if step > 0 else 0
                    wide_x[phase, :, low : low + 2] = jnp.zeros(
                        (3, 2) + velocity.shape[2:], jnp.float32
                    )
                else:
                    low = cells_y + 8 if step > 0 else 0
                    wide_y[phase, :, :, low : low + 8] = jnp.zeros(
                        (3, cells_x, 8, velocity.shape[3]), jnp.float32
                    )

    barrier = pltpu.get_barrier_semaphore()
    for axis, step in sides:

        @pl.when(present(axis, step))
        def _():
            pl.semaphore_signal(
                barrier,
                inc=1,
                device_id=neighbour(axis, step),
                device_id_type=pl.DeviceIdType.MESH,
            )

    pl.semaphore_wait(
        barrier, sum(present(axis, step).astype(jnp.int32) for axis, step in sides)
    )

    def copy_of(phase, side):
        axis, step = sides[side]
        if axis == 0:
            wide = wide_x.at[phase]
            source = wide.at[:, pl.ds(cells_x if step > 0 else 2, 2)]
            target = wide.at[:, pl.ds(0 if step > 0 else cells_x + 2, 2)]
        else:
            wide = wide_y.at[phase]
            source = wide.at[:, :, pl.ds(cells_y if step > 0 else 8, 8)]
            target = wide.at[:, :, pl.ds(0 if step > 0 else cells_y + 8, 8)]
        return pltpu.make_async_remote_copy(
            src_ref=source,
            dst_ref=target,
            send_sem=send_sem.at[phase, side],
            recv_sem=recv_sem.at[phase, side],
            device_id=neighbour(axis, step),
            device_id_type=pl.DeviceIdType.MESH,
        )

    def send(phase):
        for side, (axis, step) in enumerate(sides):

            @pl.when(present(axis, step))
            def _():
                copy_of(phase, side).start()

    def receive(phase):
        for side, (axis, step) in enumerate(sides):

            @pl.when(present(axis, -step))
            def _():
                copy_of(phase, side).wait_recv()

    def first_part(phase, part, offset):
        return wide_x[phase, part, offset : offset + cells_x]

    def second_part(phase, part, offset):
        return wide_y[phase, part, :, 6 + offset : 6 + offset + cells_y]

    def back(load, phase, part):
        return combine(*(load(phase, part, offset) for offset in (2, 1, 3, 0)))

    def ahead(load, phase, part):
        return combine(*(load(phase, part, offset) for offset in (3, 2, 4, 1)))

    def fill(phase, firsts, seconds):
        for part in range(3):
            wide_x[phase, part, 2 : 2 + cells_x] = firsts[part]
            wide_y[phase, part, :, 8 : 8 + cells_y] = seconds[part]

    for window_step in range(steps):
        held = stress if window_step == 0 else stress_out
        motion = velocity if window_step == 0 else velocity_out
        lame_from = lame_accum if window_step == 0 else lame_out
        shear_from = shear_accum if window_step == 0 else shear_out
        phase = 2 * window_step
        fill(phase, (held[0], held[3], held[4]), (held[1], held[3], held[5]))
        send(phase)
        forces = [
            third_back(held[4]),
            third_back(held[5]),
            third_ahead(held[2]) + surface[window_step],
        ]
        receive(phase)
        forces[0] += ahead(first_part, phase, 0) + back(second_part, phase, 1)
        forces[1] += back(first_part, phase, 1) + ahead(second_part, phase, 0)
        forces[2] += back(first_part, phase, 2) + back(second_part, phase, 2)
        for part in range(3):
            velocity_out[part] = motion[part] + time_step * buoyancy[...] * forces[part]
        phase += 1
        moved = [velocity_out[part] for part in range(3)]
        fill(phase, moved, moved)
        send(phase)
        rate_third = third_back(moved[2])
        shear_two = third_ahead(moved[0])
        shear_three = third_ahead(moved[1])
        receive(phase)
        rate_first = back(first_part, phase, 0)
        rate_second = back(second_part, phase, 1)
        shear_one = ahead(second_part, phase, 0) + ahead(first_part, phase, 1)
        shear_two += ahead(first_part, phase, 2)
        shear_three += ahead(second_part, phase, 2)
        dilation = rate_first + rate_second + rate_third
        spread = lame_first[...] * dilation
        stiff = shear_modulus[...]
        for part, rate in enumerate((rate_first, rate_second, rate_third)):
            stress_out[part] = held[part] + time_step * (spread + 2.0 * stiff * rate)
        for part, rate in enumerate((shear_one, shear_two, shear_three)):
            stress_out[3 + part] = held[3 + part] + time_step * (stiff * rate)
        seen = [strain[6 * window_step + part].astype(jnp.float32) for part in range(6)]
        lame_out[...] = lame_from[...] + time_step * (seen[0] + seen[1] + seen[2]) * dilation
        shear_out[...] = shear_from[...] + 2.0 * time_step * (
            seen[0] * rate_first
            + seen[1] * rate_second
            + seen[2] * rate_third
            + seen[3] * shear_one
            + seen[4] * shear_two
            + seen[5] * shear_three
        )
    for phase in range(2 * steps):
        for side, (axis, step) in enumerate(sides):

            @pl.when(present(axis, step))
            def _():
                copy_of(phase, side).wait_send()


def run_window(velocity, stress, lame_first, shear_modulus, buoyancy, strain, lame, shear, surface):
    counts = (lax.axis_size("gx"), lax.axis_size("gy"))
    steps, cells_x, cells_y, cells_z = surface.shape
    shapes = (velocity, stress, lame, shear)
    in_vmem = pl.BlockSpec(memory_space=pltpu.VMEM)
    return pl.pallas_call(
        functools.partial(stencil_kernel, counts),
        out_shape=[jax.ShapeDtypeStruct(value.shape, value.dtype) for value in shapes],
        in_specs=[in_vmem] * 9,
        out_specs=[in_vmem] * 4,
        scratch_shapes=[
            pltpu.VMEM((2 * steps, 3, cells_x + 4, cells_y, cells_z), jnp.float32),
            pltpu.VMEM((2 * steps, 3, cells_x, cells_y + 16, cells_z), jnp.float32),
            pltpu.SemaphoreType.DMA((2 * steps, 4)),
            pltpu.SemaphoreType.DMA((2 * steps, 4)),
        ],
        compiler_params=pltpu.CompilerParams(
            collective_id=0, has_side_effects=True, vmem_limit_bytes=32 * 1024 * 1024
        ),
    )(velocity, stress, lame_first, shear_modulus, buoyancy, strain, lame, shear, surface)


def split_halves(value):
    top = lax.reduce_precision(value, 8, 7)
    return top.astype(jnp.bfloat16), (value - top).astype(jnp.bfloat16)


def partner_sums(scaled, station_pairs, devices):
    stations = scaled.shape[0]
    pairs = station_pairs.shape[0]
    if stations > 1024:
        first, second = station_pairs[:, 0], station_pairs[:, 1]
        total = jnp.zeros_like(scaled).at[first].add(scaled[second])
        return total.at[second].add(scaled[first])
    held = stations // devices
    blocks = station_pairs.reshape(devices, pairs // devices, 2)
    offset = jnp.arange(devices)[:, None] * held
    first_hot = ((blocks[:, :, 0] - offset)[:, :, None] == jnp.arange(held)).astype(jnp.bfloat16)
    second_hot = (blocks[:, :, 1][:, :, None] == jnp.arange(stations)).astype(jnp.bfloat16)
    counts = (
        jnp.einsum("bpj,bpt->bjt", first_hot, second_hot, preferred_element_type=jnp.float32)
        .astype(jnp.bfloat16)
        .reshape(stations, stations)
    )
    both = jnp.concatenate(split_halves(scaled), axis=1)
    width = scaled.shape[1]
    total = lax.dot_general(
        counts, both, (((1,), (0,)), ((), ())), preferred_element_type=jnp.float32
    ) + lax.dot_general(
        counts, both, (((0,), (0,)), ((), ())), preferred_element_type=jnp.float32
    )
    return total[:, :width] + total[:, width:]


def adjoint_rows(residuals, station_pairs):
    axes = ("gx", "gy")
    held, samples = residuals.shape
    devices = lax.axis_size(axes)
    chunk = samples // devices
    values = residuals.astype(jnp.float32)
    inverse = 1.0 / jnp.sqrt(jnp.mean(values * values, axis=1, keepdims=True) + epsilon)
    inverse_top, inverse_rest = split_halves(inverse.reshape(1, held))
    scales = jnp.concatenate([inverse_top, inverse_rest], axis=0)
    scales = jnp.pad(scales, ((0, 14), (0, chunk - held)))
    payload = jnp.concatenate(
        [
            residuals.reshape(held, devices, chunk).transpose(1, 0, 2),
            jnp.broadcast_to(scales[None], (devices, 16, chunk)),
        ],
        axis=1,
    )
    arrived = lax.all_to_all(payload, axes, split_axis=0, concat_axis=0, tiled=True)
    arrived_scales = arrived[:, held, :held].astype(jnp.float32) + arrived[
        :, held + 1, :held
    ].astype(jnp.float32)
    scaled = (arrived[:, :held].astype(jnp.float32) * arrived_scales[:, :, None]).reshape(
        devices * held, chunk
    )
    sums = partner_sums(scaled, station_pairs, devices).reshape(devices, held, chunk)
    back = lax.all_to_all(sums, axes, split_axis=0, concat_axis=0, tiled=True)
    back = back.transpose(1, 0, 2).reshape(held, samples)
    normed = values * inverse
    corr_sum = jnp.mean(normed * back, axis=1, keepdims=True)
    return back - corr_sum * normed


def shards(
    velocity,
    stress,
    lame_first,
    shear_modulus,
    buoyancy,
    forward_strain,
    lame_accum,
    shear_accum,
    residuals,
    station_cell,
    station_pairs,
):
    samples = residuals.shape[1]
    adjoint = adjoint_rows(residuals, station_pairs)
    cells_first = velocity.shape[1]
    cells_second = velocity.shape[2]
    step_count = forward_strain.shape[0] // 6
    cells_hit = (station_cell[:, None] == jnp.arange(cells_first * cells_second)[None, :]).astype(
        jnp.float32
    )
    surfaces = jnp.stack(
        [
            jnp.sum(cells_hit * adjoint[:, samples - 1 - window_step][:, None], axis=0).reshape(
                cells_first, cells_second
            )
            for window_step in range(step_count)
        ]
    )
    deep = lax.broadcasted_iota(jnp.int32, surfaces.shape + (velocity.shape[3],), 3)
    surface = jnp.where(deep == 0, surfaces[..., None], 0.0)
    velocity, stress, lame_accum, shear_accum = run_window(
        velocity,
        stress,
        lame_first,
        shear_modulus,
        buoyancy,
        forward_strain,
        lame_accum,
        shear_accum,
        surface,
    )
    return (velocity, stress, lame_accum, shear_accum, adjoint)


def solution(mesh):
    return jax.shard_map(
        shards,
        mesh=mesh,
        in_specs=(
            P(None, "gx", "gy", None),
            P(None, "gx", "gy", None),
            P("gx", "gy", None),
            P("gx", "gy", None),
            P("gx", "gy", None),
            P(None, "gx", "gy", None),
            P("gx", "gy", None),
            P("gx", "gy", None),
            P(("gx", "gy"), None),
            P(("gx", "gy")),
            P(),
        ),
        out_specs=(
            P(None, "gx", "gy", None),
            P(None, "gx", "gy", None),
            P("gx", "gy", None),
            P("gx", "gy", None),
            P(("gx", "gy"), None),
        ),
        check_vma=False,
    )
```

time: 105 us -> 66 us (0.63)
  the two profiles are of different devices: /device:TPU:6 before, /device:TPU:0 now
where the time goes in v2:
time: 66 us; the launch traced here: 65.7 us
  waiting for transfers between devices  25 us (38%)
  Pallas kernels  16.7 us (25%)
  starting transfers between devices  9.94 us (15%)
  matrix products  5.09 us (8%)
  local copies, waits for them, and re-layouts  5.01 us (8%)
  other arithmetic  3.03 us (5%)
  between operations  0.95 us (1%)
    pallas_call x1, Pallas kernels, run_window(): pl.pallas_call(functools.partial(stencil_kernel, counts), out_shape=[jax....  16.7 us
    all_to_all x1, waiting for transfers between devices, adjoint_rows(): back = lax.all_to_all(sums, axes, split_axis=0, concat_axis=0, tiled=True)  15.5 us
    all_to_all x1, waiting for transfers between devices, adjoint_rows(): lax.all_to_all(payload, axes, split_axis=0, concat_axis=0, tiled=True)  9.42 us
    all_to_all x1, starting transfers between devices, adjoint_rows(): lax.all_to_all(payload, axes, split_axis=0, concat_axis=0, tiled=True)  7.3 us
    unnamed x30, local copies, waits for them, and re-layouts  3.76 us
    dot_general x1, matrix products, partner_sums(): jnp.einsum('bpj,bpt->bjt', first_hot, second_hot, preferred_element_type=...  3.65 us
    all_to_all x1, starting transfers between devices, adjoint_rows(): back = lax.all_to_all(sums, axes, split_axis=0, concat_axis=0, tiled=True)  2.64 us
  transfers between devices with their start and end apart: 2, of which 2 were waited for; matrix products, arithmetic and copies ran while one was open for 6% of the time, Pallas kernels for 0%

profile of v2, /device:TPU:0, one launch (start us, length us, event | category | flops | bytes accessed | tf_op | source)
XLA Modules:
  0.0 65.7 jit_solution(15957329807007730248)
XLA Ops:
  0.6 1.1 %fusion.7 = f32[32]{0:T(128)S(1)} fusion(bf16[32,4096]{1,0:T(8,128)(2,1)} %param.19), kind=kLoop, calls=%fused_computation.13 | loop fusion | flops 393184 | bytes 262272 | tf_op jit(solution)/shard_map/reduce_sum | solution.py:267
  1.8 1.0 %copy.28 = bf16[4,8,32,128]{3,2,1,0:T(8,128)(2,1)S(1)} copy(bf16[4,8,32,128]{3,1,2,0:T(8,128)(2,1)} %bitcast.34) | data formatting | bytes 524288
  2.9 0.9 %copy.24 = bf16[32,48,128]{2,1,0:T(8,128)(2,1)} copy(bf16[32,48,128]{2,0,1:T(8,128)(2,1)S(1)} %pad_maximum_fusion.1) | data formatting | bytes 786432 | tf_op jit(solution)/shard_map/concatenate | solution.py:271
  3.8 7.3 %all-to-all-start = ((bf16[32,48,128]{2,1,0:T(8,128)(2,1)}), bf16[32,48,128]{2,1,0:T(8,128)(2,1)S(1)}, u32[]{:S(2)}, u32[]{:S(2)}) async-start(bf16[32,48,128]{2,1,0:T(8,128)(2,1)} %copy.24), calls=%async_computation | async-start | bytes 786432 | tf_op jit(solution)/shard_map/all_to_all | solution.py:278
  11.2 3.6 %fusion.2 = bf16[32,32,1024]{2,1,0:T(8,128)(2,1)S(1)} fusion(s32[32,128]{1,0:T(8,128)S(1)} %get-tuple-element.22, s32[32,128]{1,0:T(8,128)S(1)} %get-tuple-element.21), kind=kOutput, calls=%fused_computation.3 | convolution fusion | flops 273809408 | bytes 2129920 | tf_op jit(solution)/shard_map/bpj,bpt->bjt/dot_general | solution.py:247
  14.8 9.4 %all-to-all-done = bf16[32,48,128]{2,1,0:T(8,128)(2,1)S(1)} async-done(((bf16[32,48,128]{2,1,0:T(8,128)(2,1)}), bf16[32,48,128]{2,1,0:T(8,128)(2,1)S(1)}, u32[]{:S(2)}, u32[]{:S(2)}) %all-to-all-start) | async-done | bytes 393248 | tf_op jit(solution)/shard_map/all_to_all | solution.py:278
  24.3 0.2 convert_multiply_fusion.2
  24.5 0.1 reduce-precision_convert_fusion
  24.6 0.7 %fusion.9 = f32[1024,256]{1,0:T(8,128)S(1)} fusion(bf16[1024,1024]{1,0:T(8,128)(2,1)S(1)} %bitcast.39, bf16[1024,128]{1,0:T(8,128)(2,1)S(1)} %get-tuple-element.20, bf16[1024,128]{1,0:T(8,128)(2,1)S(1)} %get-tuple-element.19), kind=kOutput, calls=%fused_computation.20 | convolution fusion | flops 537919488 | bytes 3670016 | tf_op jit(solution)/shard_map/dot_general | solution.py:253
  25.3 0.7 %convolution_add_fusion = f32[1024,256]{1,0:T(8,128)S(1)} fusion(f32[1024,256]{1,0:T(8,128)S(1)} %fusion.9, bf16[1024,1024]{1,0:T(8,128)(2,1)S(1)} %bitcast.40, bf16[1024,128]{1,0:T(8,128)(2,1)S(1)} %get-tuple-element.20, bf16[1024,128]{1,0:T(8,128)(2,1)S(1)} %get-tuple-element.19), kind=kOutput, calls=%fused_computation.4 | convolution fusion | flops 538181632 | bytes 4718592 | tf_op jit(solution)/shard_map/dot_general | solution.py:255
  26.2 0.8 %slice_add_fusion = f32[1024,128]{1,0:T(8,128)} fusion(f32[1024,256]{1,0:T(8,128)S(1)} %convolution_add_fusion), kind=kLoop, calls=%fused_computation.15 | loop fusion | flops 131072 | bytes 1572864 | tf_op jit(solution)/shard_map/add | solution.py:258
  27.0 2.6 %all-to-all-start.1 = ((f32[32,32,128]{2,1,0:T(8,128)}), f32[32,32,128]{2,1,0:T(8,128)S(1)}, u32[]{:S(2)}, u32[]{:S(2)}) async-start(f32[32,32,128]{2,1,0:T(8,128)} %bitcast.7), calls=%async_computation.1 | async-start | bytes 1048576 | tf_op jit(solution)/shard_map/all_to_all | solution.py:286
  29.7 15.5 %all-to-all-done.1 = f32[32,32,128]{2,1,0:T(8,128)S(1)} async-done(((f32[32,32,128]{2,1,0:T(8,128)}), f32[32,32,128]{2,1,0:T(8,128)S(1)}, u32[]{:S(2)}, u32[]{:S(2)}) %all-to-all-start.1) | async-done | bytes 524320 | tf_op jit(solution)/shard_map/all_to_all | solution.py:286
  45.2 0.3 fusion.5
  45.5 0.1 fusion.6
  45.6 0.2 slice_reduce_fusion.1
  45.8 0.1 select_reduce_fusion.1
  45.9 0.1 stack_reshape.6
  46.1 0.1 broadcast_select_fusion.surface
  46.3 16.7 %shard_map.146 = (f32[3,8,16,128]{3,2,1,0:T(8,128)S(1)}, f32[6,8,16,128]{3,2,1,0:T(8,128)S(1)}, f32[8,16,128]{2,1,0:T(8,128)S(1)}, f32[8,16,128]{2,1,0:T(8,128)S(1)}) custom-call(f32[3,8,16,128]{3,2,1,0:T(8,128)S(1)} %copy-done.2, f32[6,8,16,128]{3,2,1,0:T(8,128)S(1)} %copy-done, f32[8,16,128]{2,1,0:T(8,128)S(1)} %copy-done.3, f32[8,16,128]{2,1,0:T(8,128)S(1)} %copy-done.4, ...), custom_call_target="tpu_custom_call" | custom-call | tf_op jit(solution)/shard_map/pallas_call | solution.py:212
  63.0 0.7 %copy.37 = f32[3,8,16,128]{3,2,1,0:T(8,128)} copy(f32[3,8,16,128]{3,2,1,0:T(8,128)S(1)} %get-tuple-element.28) | data formatting | bytes 393216
  63.7 0.7 %copy.38 = f32[6,8,16,128]{3,2,1,0:T(8,128)} copy(f32[6,8,16,128]{3,2,1,0:T(8,128)S(1)} %get-tuple-element.29) | data formatting | bytes 786432
  64.4 0.6 copy.39
  65.0 0.6 copy.40
  (37 shorter events, 0.4 us)
Async XLA Ops:
  0.6 10.4 %copy-start.10 = (s32[4096,2]{0,1:T(2,128)S(1)}, s32[4096,2]{0,1:T(2,128)}, u32[]{:S(2)}) copy-start(s32[4096,2]{0,1:T(2,128)} %param.21) | copy-start | bytes 98308
  3.8 20.5 %all-to-all-start = ((bf16[32,48,128]{2,1,0:T(8,128)(2,1)}), bf16[32,48,128]{2,1,0:T(8,128)(2,1)S(1)}, u32[]{:S(2)}, u32[]{:S(2)}) async-start(bf16[32,48,128]{2,1,0:T(8,128)(2,1)} %copy.24), calls=%async_computation | async-start | bytes 786432 | tf_op jit(solution)/shard_map/all_to_all | solution.py:278
  26.0 19.2 %copy-start.8 = (bf16[32,4096]{1,0:T(8,128)(2,1)S(1)}, bf16[32,4096]{1,0:T(8,128)(2,1)}, u32[]{:S(2)}) copy-start(bf16[32,4096]{1,0:T(8,128)(2,1)} %param.19) | copy-start | bytes 786436
  26.1 19.8 %copy-start.11 = (s32[32]{0:T(128)S(1)}, s32[32]{0:T(128)}, u32[]{:S(2)}) copy-start(s32[32]{0:T(128)} %param.20) | copy-start | bytes 388
  26.1 20.1 %copy-start = (f32[6,8,16,128]{3,2,1,0:T(8,128)S(1)}, f32[6,8,16,128]{3,2,1,0:T(8,128)}, u32[]{:S(2)}) copy-start(f32[6,8,16,128]{3,2,1,0:T(8,128)} %stress.1) | copy-start | bytes 1179652
  26.1 20.1 %copy-start.1 = (bf16[12,8,16,128]{3,2,1,0:T(8,128)(2,1)S(1)}, bf16[12,8,16,128]{3,2,1,0:T(8,128)(2,1)}, u32[]{:S(2)}) copy-start(bf16[12,8,16,128]{3,2,1,0:T(8,128)(2,1)} %strain.1) | copy-start | bytes 1179652
  26.1 20.1 %copy-start.2 = (f32[3,8,16,128]{3,2,1,0:T(8,128)S(1)}, f32[3,8,16,128]{3,2,1,0:T(8,128)}, u32[]{:S(2)}) copy-start(f32[3,8,16,128]{3,2,1,0:T(8,128)} %velocity.1) | copy-start | bytes 589828
  26.1 20.1 %copy-start.3 = (f32[8,16,128]{2,1,0:T(8,128)S(1)}, f32[8,16,128]{2,1,0:T(8,128)}, u32[]{:S(2)}) copy-start(f32[8,16,128]{2,1,0:T(8,128)} %lame_first.1) | copy-start | bytes 196612
  26.1 20.1 %copy-start.4 = (f32[8,16,128]{2,1,0:T(8,128)S(1)}, f32[8,16,128]{2,1,0:T(8,128)}, u32[]{:S(2)}) copy-start(f32[8,16,128]{2,1,0:T(8,128)} %shear_modulus.1) | copy-start | bytes 196612
  26.1 20.1 %copy-start.5 = (f32[8,16,128]{2,1,0:T(8,128)S(1)}, f32[8,16,128]{2,1,0:T(8,128)}, u32[]{:S(2)}) copy-start(f32[8,16,128]{2,1,0:T(8,128)} %buoyancy.1) | copy-start | bytes 196612
  26.1 20.1 %copy-start.6 = (f32[8,16,128]{2,1,0:T(8,128)S(1)}, f32[8,16,128]{2,1,0:T(8,128)}, u32[]{:S(2)}) copy-start(f32[8,16,128]{2,1,0:T(8,128)} %lame_accum.1) | copy-start | bytes 196612
  26.1 20.1 %copy-start.7 = (f32[8,16,128]{2,1,0:T(8,128)S(1)}, f32[8,16,128]{2,1,0:T(8,128)}, u32[]{:S(2)}) copy-start(f32[8,16,128]{2,1,0:T(8,128)} %shear_accum.1) | copy-start | bytes 196612
  27.0 18.2 %all-to-all-start.1 = ((f32[32,32,128]{2,1,0:T(8,128)}), f32[32,32,128]{2,1,0:T(8,128)S(1)}, u32[]{:S(2)}, u32[]{:S(2)}) async-start(f32[32,32,128]{2,1,0:T(8,128)} %bitcast.7), calls=%async_computation.1 | async-start | bytes 1048576 | tf_op jit(solution)/shard_map/all_to_all | solution.py:286
  45.6 20.1 %copy-start.9 = (f32[32,4096]{1,0:T(8,128)}, f32[32,4096]{1,0:T(8,128)S(1)}, u32[]{:S(2)}) copy-start(f32[32,4096]{1,0:T(8,128)S(1)} %fusion.6) | copy-start | bytes 1572868

commit v3 on v2

--- a/solution.py
+++ b/solution.py
@@ -34,6 +34,7 @@
 
 def stencil_kernel(
     counts,
+    fused,
     velocity,
     stress,
     lame_first,
@@ -42,17 +43,16 @@
     strain,
     lame_accum,
     shear_accum,
-    surface,
-    velocity_out,
-    stress_out,
-    lame_out,
-    shear_out,
-    wide_x,
-    wide_y,
-    send_sem,
-    recv_sem,
+    *rest,
 ):
-    steps = surface.shape[0]
+    if fused:
+        sums, residuals, inverse, hits = rest[:4]
+        velocity_out, stress_out, lame_out, shear_out, adjoint = rest[4:9]
+        wide_x, wide_y, send_sem, recv_sem, back_rows, fields, sum_send, sum_recv = rest[9:]
+    else:
+        surface, velocity_out, stress_out, lame_out, shear_out = rest[:5]
+        wide_x, wide_y, send_sem, recv_sem = rest[5:]
+    steps = strain.shape[0] // 6
     cells_x, cells_y = velocity.shape[1], velocity.shape[2]
     place = (lax.axis_index("gx"), lax.axis_index("gy"))
 
@@ -82,20 +82,84 @@
                     )
 
     barrier = pltpu.get_barrier_semaphore()
-    for axis, step in sides:
-
-        @pl.when(present(axis, step))
-        def _():
+    devices = counts[0] * counts[1]
+    mine = place[0] * counts[1] + place[1]
+    if fused:
+
+        def greet(hop, carry):
+            other = lax.rem(mine + hop, devices)
             pl.semaphore_signal(
                 barrier,
                 inc=1,
-                device_id=neighbour(axis, step),
+                device_id=(other // counts[1], lax.rem(other, counts[1])),
                 device_id_type=pl.DeviceIdType.MESH,
             )
-
-    pl.semaphore_wait(
-        barrier, sum(present(axis, step).astype(jnp.int32) for axis, step in sides)
-    )
+            return carry
+
+        lax.fori_loop(1, devices, greet, 0)
+        pl.semaphore_wait(barrier, devices - 1)
+    else:
+        for axis, step in sides:
+
+            @pl.when(present(axis, step))
+            def _():
+                pl.semaphore_signal(
+                    barrier,
+                    inc=1,
+                    device_id=neighbour(axis, step),
+                    device_id_type=pl.DeviceIdType.MESH,
+                )
+
+        pl.semaphore_wait(
+            barrier, sum(present(axis, step).astype(jnp.int32) for axis, step in sides)
+        )
+
+    def sum_copy(owner, target):
+        return pltpu.make_async_remote_copy(
+            src_ref=sums.at[target],
+            dst_ref=back_rows.at[owner],
+            send_sem=sum_send.at[target],
+            recv_sem=sum_recv.at[owner],
+            device_id=(target // counts[1], lax.rem(target, counts[1])),
+            device_id_type=pl.DeviceIdType.MESH,
+        )
+
+    def start_sums():
+        def start_one(hop, carry):
+            sum_copy(mine, lax.rem(mine + hop, devices)).start()
+            return carry
+
+        lax.fori_loop(1, devices, start_one, 0)
+        back_rows[pl.ds(mine, 1)] = sums[pl.ds(mine, 1)]
+
+    def finish_sums():
+        def wait_one(hop, carry):
+            other = lax.rem(mine + hop, devices)
+            sum_copy(other, other).wait_recv()
+            return carry
+
+        lax.fori_loop(1, devices, wait_one, 0)
+        held_rows, width = back_rows.shape[1], back_rows.shape[2]
+        scale = inverse[...]
+        total = jnp.zeros((held_rows, width), jnp.float32)
+        for part in range(devices):
+            normed = residuals[:, part * width : (part + 1) * width].astype(jnp.float32) * scale
+            total = total + normed * back_rows[part]
+        corr_sum = jnp.sum(total, axis=1, keepdims=True) * (1.0 / (devices * width))
+        for part in range(devices):
+            normed = residuals[:, part * width : (part + 1) * width].astype(jnp.float32) * scale
+            last = back_rows[part] - corr_sum * normed
+            adjoint[:, part * width : (part + 1) * width] = last
+        station = lax.broadcasted_iota(jnp.int32, last.shape, 0)
+        lane = lax.broadcasted_iota(jnp.int32, last.shape, 1)
+        depth = lax.broadcasted_iota(jnp.int32, hits.shape, 2)
+        for window_step in range(steps):
+            column = jnp.sum(
+                jnp.where(lane == width - 1 - window_step, last, 0.0), axis=1, keepdims=True
+            )
+            row = jnp.sum(jnp.where(station == lane, column, 0.0), axis=0, keepdims=True)
+            cells = jnp.sum(hits[...] * row[None], axis=2, keepdims=True)
+            fields[window_step] = jnp.where(depth == 0, cells, 0.0)
 
     def copy_of(phase, side):
         axis, step = sides[side]
@@ -155,17 +219,22 @@
         phase = 2 * window_step
         fill(phase, (held[0], held[3], held[4]), (held[1], held[3], held[5]))
         send(phase)
-        forces = [
-            third_back(held[4]),
-            third_back(held[5]),
-            third_ahead(held[2]) + surface[window_step],
-        ]
+        if fused and window_step == 0:
+            start_sums()
+        forces = [third_back(held[4]), third_back(held[5]), third_ahead(held[2])]
+        if not fused:
+            forces[2] += surface[window_step]
+        elif window_step > 0:
+            forces[2] += fields[window_step]
         receive(phase)
         forces[0] += ahead(first_part, phase, 0) + back(second_part, phase, 1)
         forces[1] += back(first_part, phase, 1) + ahead(second_part, phase, 0)
         forces[2] += back(first_part, phase, 2) + back(second_part, phase, 2)
         for part in range(3):
             velocity_out[part] = motion[part] + time_step * buoyancy[...] * forces[part]
+        if fused and window_step == 0:
+            finish_sums()
+            velocity_out[2] += time_step * buoyancy[...] * fields[0]
         phase += 1
         moved = [velocity_out[part] for part in range(3)]
         fill(phase, moved, moved)
@@ -203,27 +272,50 @@
             def _():
                 copy_of(phase, side).wait_send()
 
-
-def run_window(velocity, stress, lame_first, shear_modulus, buoyancy, strain, lame, shear, surface):
+    if fused:
+
+        def wait_sent(hop, carry):
+            other = lax.rem(mine + hop, devices)
+            sum_copy(mine, other).wait_send()
+            return carry
+
+        lax.fori_loop(1, devices, wait_sent, 0)
+
+
+def run_window(velocity, stress, lame_first, shear_modulus, buoyancy, strain, lame, shear, extra):
     counts = (lax.axis_size("gx"), lax.axis_size("gy"))
-    steps, cells_x, cells_y, cells_z = surface.shape
-    shapes = (velocity, stress, lame, shear)
+    devices = counts[0] * counts[1]
+    fused = len(extra) > 1
+    cells_x, cells_y, cells_z = velocity.shape[1:]
+    steps = strain.shape[0] // 6
+    shapes = [
+        jax.ShapeDtypeStruct(value.shape, value.dtype) for value in (velocity, stress, lame, shear)
+    ]
+    scratch = [
+        pltpu.VMEM((2 * steps, 3, cells_x + 4, cells_y, cells_z), jnp.float32),
+        pltpu.VMEM((2 * steps, 3, cells_x, cells_y + 16, cells_z), jnp.float32),
+        pltpu.SemaphoreType.DMA((2 * steps, 4)),
+        pltpu.SemaphoreType.DMA((2 * steps, 4)),
+    ]
+    if fused:
+        shapes.append(jax.ShapeDtypeStruct(extra[1].shape, jnp.float32))
+        scratch += [
+            pltpu.VMEM(extra[0].shape, jnp.float32),
+            pltpu.VMEM((steps, cells_x, cells_y, cells_z), jnp.float32),
+            pltpu.SemaphoreType.DMA((devices,)),
+            pltpu.SemaphoreType.DMA((devices,)),
+        ]
     in_vmem = pl.BlockSpec(memory_space=pltpu.VMEM)
     return pl.pallas_call(
-        functools.partial(stencil_kernel, counts),
-        out_shape=[jax.ShapeDtypeStruct(value.shape, value.dtype) for value in shapes],
-        in_specs=[in_vmem] * 9,
-        out_specs=[in_vmem] * 4,
-        scratch_shapes=[
-            pltpu.VMEM((2 * steps, 3, cells_x + 4, cells_y, cells_z), jnp.float32),
-            pltpu.VMEM((2 * steps, 3, cells_x, cells_y + 16, cells_z), jnp.float32),
-            pltpu.SemaphoreType.DMA((2 * steps, 4)),
-            pltpu.SemaphoreType.DMA((2 * steps, 4)),
-        ],
+        functools.partial(stencil_kernel, counts, fused),
+        out_shape=shapes,
+        in_specs=[in_vmem] * (8 + len(extra)),
+        out_specs=[in_vmem] * len(shapes),
+        scratch_shapes=scratch,
         compiler_params=pltpu.CompilerParams(
             collective_id=0, has_side_effects=True, vmem_limit_bytes=32 * 1024 * 1024
         ),
-    )(velocity, stress, lame_first, shear_modulus, buoyancy, strain, lame, shear, surface)
+    )(velocity, stress, lame_first, shear_modulus, buoyancy, strain, lame, shear, *extra)
 
 
 def split_halves(value):
@@ -258,7 +350,7 @@
     return total[:, :width] + total[:, width:]
 
 
-def adjoint_rows(residuals, station_pairs):
+def shard_sums(residuals, station_pairs):
     axes = ("gx", "gy")
     held, samples = residuals.shape
     devices = lax.axis_size(axes)
@@ -283,6 +375,13 @@
         devices * held, chunk
     )
     sums = partner_sums(scaled, station_pairs, devices).reshape(devices, held, chunk)
+    return sums, inverse
+
+
+def adjoint_rows(sums, residuals, inverse):
+    axes = ("gx", "gy")
+    held, samples = residuals.shape
+    values = residuals.astype(jnp.float32)
     back = lax.all_to_all(sums, axes, split_axis=0, concat_axis=0, tiled=True)
     back = back.transpose(1, 0, 2).reshape(held, samples)
     normed = values * inverse
@@ -304,24 +403,8 @@
     station_pairs,
 ):
     samples = residuals.shape[1]
-    adjoint = adjoint_rows(residuals, station_pairs)
-    cells_first = velocity.shape[1]
-    cells_second = velocity.shape[2]
-    step_count = forward_strain.shape[0] // 6
-    cells_hit = (station_cell[:, None] == jnp.arange(cells_first * cells_second)[None, :]).astype(
-        jnp.float32
-    )
-    surfaces = jnp.stack(
-        [
-            jnp.sum(cells_hit * adjoint[:, samples - 1 - window_step][:, None], axis=0).reshape(
-                cells_first, cells_second
-            )
-            for window_step in range(step_count)
-        ]
-    )
-    deep = lax.broadcasted_iota(jnp.int32, surfaces.shape + (velocity.shape[3],), 3)
-    surface = jnp.where(deep == 0, surfaces[..., None], 0.0)
-    velocity, stress, lame_accum, shear_accum = run_window(
+    sums, inverse = shard_sums(residuals, station_pairs)
+    fields = (
         velocity,
         stress,
         lame_first,
@@ -330,9 +413,31 @@
         forward_strain,
         lame_accum,
         shear_accum,
-        surface,
-    )
-    return (velocity, stress, lame_accum, shear_accum, adjoint)
+    )
+    if sums.shape[2] % 128 == 0 and sums.shape[2] == velocity.shape[3]:
+        cells = velocity.shape[1] * velocity.shape[2]
+        stations = jnp.pad(station_cell, (0, sums.shape[2] - sums.shape[1]), constant_values=-1)
+        hits = (jnp.arange(cells)[:, None] == stations[None, :]).astype(jnp.float32)
+        hits = hits.reshape(velocity.shape[1:3] + (sums.shape[2],))
+        return tuple(run_window(*fields, (sums, residuals, inverse, hits)))
+    adjoint = adjoint_rows(sums, residuals, inverse)
+    cells_first = velocity.shape[1]
+    cells_second = velocity.shape[2]
+    step_count = forward_strain.shape[0] // 6
+    cells_hit = (station_cell[:, None] == jnp.arange(cells_first * cells_second)[None, :]).astype(
+        jnp.float32
+    )
+    surfaces = jnp.stack(
+        [
+            jnp.sum(cells_hit * adjoint[:, samples - 1 - window_step][:, None], axis=0).reshape(
+                cells_first, cells_second
+            )
+            for window_step in range(step_count)
+        ]
+    )
+    deep = lax.broadcasted_iota(jnp.int32, surfaces.shape + (velocity.shape[3],), 3)
+    surface = jnp.where(deep == 0, surfaces[..., None], 0.0)
+    return (*run_window(*fields, (surface,)), adjoint)
 
 
 def solution(mesh):

time: 66 us -> 59.9 us (0.908)
  waiting for transfers between devices: 25 us -> 9.19 us
  Pallas kernels: 16.7 us -> 29.5 us
  starting transfers between devices: 9.94 us -> 7.3 us
  other arithmetic: 3.03 us -> 1.71 us
  local copies, waits for them, and re-layouts: 5.01 us -> 5.92 us
    all_to_all x2 -> x1, waiting for transfers between devices: 25 us -> 9.19 us  [shard_sums(): lax.all_to_all(payload, axes, split_axis=0, concat_axis=0, tiled=True)]
    pallas_call x1, Pallas kernels: 16.7 us -> 29.5 us  [run_window(): pl.pallas_call(functools.partial(stencil_kernel, counts, fused), out_shap...]
    all_to_all x2 -> x1, starting transfers between devices: 9.94 us -> 7.3 us  [shard_sums(): lax.all_to_all(payload, axes, split_axis=0, concat_axis=0, tiled=True)]
    unnamed x30 -> x29, local copies, waits for them, and re-layouts: 3.76 us -> 4.91 us
    add x1, other arithmetic: 0.85 us -> 0.05 us  [partner_sums(): return total[:, :width] + total[:, width:]]
    reduce_sum x3 -> x1, other arithmetic: 1.46 us -> 1.12 us  [shard_sums(): jnp.mean(values * values, axis=1, keepdims=True) + epsilon]
  transfers between devices with their start and end apart: 2 -> 1, of which waited for: 2 -> 1; matrix products, arithmetic and copies ran while one was open for 6% -> 7% of each run, Pallas kernels for 0% -> 0%
where the time goes in v3:
time: 59.9 us; the launch traced here: 59.6 us
  Pallas kernels  29.5 us (49%)
  waiting for transfers between devices  9.19 us (15%)
  starting transfers between devices  7.3 us (12%)
  local copies, waits for them, and re-layouts  5.92 us (10%)
  matrix products  5.12 us (9%)
  other arithmetic  1.71 us (3%)
  between operations  0.87 us (1%)
    pallas_call x1, Pallas kernels, run_window(): pl.pallas_call(functools.partial(stencil_kernel, counts, fused), out_shap...  29.5 us
    all_to_all x1, waiting for transfers between devices, shard_sums(): lax.all_to_all(payload, axes, split_axis=0, concat_axis=0, tiled=True)  9.19 us
    all_to_all x1, starting transfers between devices, shard_sums(): lax.all_to_all(payload, axes, split_axis=0, concat_axis=0, tiled=True)  7.3 us
    unnamed x29, local copies, waits for them, and re-layouts  4.91 us
    dot_general x1, matrix products, partner_sums(): jnp.einsum('bpj,bpt->bjt', first_hot, second_hot, preferred_element_type=...  3.66 us
  transfers between devices with their start and end apart: 1, of which 1 were waited for; matrix products, arithmetic and copies ran while one was open for 7% of the time, Pallas kernels for 0%

profile of v3, /device:TPU:0, one launch (start us, length us, event | category | flops | bytes accessed | tf_op | source)
XLA Modules:
  0.0 59.6 jit_solution(12554290605107766241)
XLA Ops:
  0.7 1.1 %multiply_reduce_fusion = f32[32]{0:T(128)S(1)} fusion(bf16[32,4096]{1,0:T(8,128)(2,1)} %rest_1_.1), kind=kLoop, calls=%fused_computation.11 | loop fusion | flops 393184 | bytes 262272 | tf_op jit(solution)/shard_map/reduce_sum | solution.py:359
  1.8 1.0 %copy.25 = bf16[4,8,32,128]{3,2,1,0:T(8,128)(2,1)S(1)} copy(bf16[4,8,32,128]{3,1,2,0:T(8,128)(2,1)} %bitcast.27) | data formatting | bytes 524288
  2.9 0.9 %copy.22 = bf16[32,48,128]{2,1,0:T(8,128)(2,1)} copy(bf16[32,48,128]{2,0,1:T(8,128)(2,1)S(1)} %pad_maximum_fusion.1) | data formatting | bytes 786432 | tf_op jit(solution)/shard_map/concatenate | solution.py:363
  3.8 7.3 %all-to-all-start = ((bf16[32,48,128]{2,1,0:T(8,128)(2,1)}), bf16[32,48,128]{2,1,0:T(8,128)(2,1)S(1)}, u32[]{:S(2)}, u32[]{:S(2)}) async-start(bf16[32,48,128]{2,1,0:T(8,128)(2,1)} %copy.22), calls=%async_computation | async-start | bytes 786432 | tf_op jit(solution)/shard_map/all_to_all | solution.py:370
  11.1 0.1 copy.23.rest_2_
  11.2 0.1 fusion.7
  11.3 0.1 compare_convert_fusion.rest_3_
  11.4 3.7 %fusion.2 = bf16[32,32,1024]{2,1,0:T(8,128)(2,1)S(1)} fusion(s32[32,128]{1,0:T(8,128)S(1)} %get-tuple-element.8, s32[32,128]{1,0:T(8,128)S(1)} %get-tuple-element.7), kind=kOutput, calls=%fused_computation.3 | convolution fusion | flops 273809408 | bytes 2129920 | tf_op jit(solution)/shard_map/bpj,bpt->bjt/dot_general | solution.py:339
  15.1 9.2 %all-to-all-done = bf16[32,48,128]{2,1,0:T(8,128)(2,1)S(1)} async-done(((bf16[32,48,128]{2,1,0:T(8,128)(2,1)}), bf16[32,48,128]{2,1,0:T(8,128)(2,1)S(1)}, u32[]{:S(2)}, u32[]{:S(2)}) %all-to-all-start) | async-done | bytes 393248 | tf_op jit(solution)/shard_map/all_to_all | solution.py:370
  24.3 0.2 convert_multiply_fusion
  24.5 0.1 reduce-precision_convert_fusion
  24.6 0.7 %fusion.4 = f32[1024,256]{1,0:T(8,128)S(1)} fusion(bf16[1024,1024]{1,0:T(8,128)(2,1)S(1)} %bitcast.33, bf16[1024,128]{1,0:T(8,128)(2,1)S(1)} %get-tuple-element.6, bf16[1024,128]{1,0:T(8,128)(2,1)S(1)} %get-tuple-element.5), kind=kOutput, calls=%fused_computation.14 | convolution fusion | flops 537919488 | bytes 3670016 | tf_op jit(solution)/shard_map/dot_general | solution.py:345
  25.4 0.7 %convolution_add_fusion = f32[1024,256]{1,0:T(8,128)S(1)} fusion(f32[1024,256]{1,0:T(8,128)S(1)} %fusion.4, bf16[1024,1024]{1,0:T(8,128)(2,1)S(1)} %bitcast.34, bf16[1024,128]{1,0:T(8,128)(2,1)S(1)} %get-tuple-element.6, bf16[1024,128]{1,0:T(8,128)(2,1)S(1)} %get-tuple-element.5), kind=kOutput, calls=%fused_computation.4 | convolution fusion | flops 538181632 | bytes 4718592 | tf_op jit(solution)/shard_map/dot_general | solution.py:347
  26.2 0.1 slice_add_fusion
  26.2 0.0 copy-done
  26.3 0.1 copy-done.1
  26.4 0.1 copy-done.2
  26.5 0.0 copy-done.3
  26.6 29.5 %shard_map.146 = (f32[3,8,16,128]{3,2,1,0:T(8,128)S(1)}, f32[6,8,16,128]{3,2,1,0:T(8,128)S(1)}, f32[8,16,128]{2,1,0:T(8,128)S(1)}, f32[8,16,128]{2,1,0:T(8,128)S(1)}, f32[32,4096]{1,0:T(8,128)S(1)}) custom-call(f32[3,8,16,128]{3,2,1,0:T(8,128)S(1)} %copy-done.3, f32[6,8,16,128]{3,2,1,0:T(8,128)S(1)} %copy-done.1, f32[8,16,128]{2,1,0:T(8,128)S(1)} %copy-done.4, ...), custom_call_target="tpu_custom_call" | custom-call | tf_op jit(solution)/shard_map/pallas_call | solution.py:309
  56.1 0.7 %copy.33 = f32[3,8,16,128]{3,2,1,0:T(8,128)} copy(f32[3,8,16,128]{3,2,1,0:T(8,128)S(1)} %get-tuple-element.16) | data formatting | bytes 393216
  56.8 0.7 %copy.34 = f32[6,8,16,128]{3,2,1,0:T(8,128)} copy(f32[6,8,16,128]{3,2,1,0:T(8,128)S(1)} %get-tuple-element.17) | data formatting | bytes 786432
  57.6 0.6 %copy.35 = f32[8,16,128]{2,1,0:T(8,128)} copy(f32[8,16,128]{2,1,0:T(8,128)S(1)} %get-tuple-element.18) | data formatting | bytes 131072
  58.2 0.6 %copy.36 = f32[8,16,128]{2,1,0:T(8,128)} copy(f32[8,16,128]{2,1,0:T(8,128)S(1)} %get-tuple-element.19) | data formatting | bytes 131072
  58.8 0.8 %copy.37 = f32[32,4096]{1,0:T(8,128)} copy(f32[32,4096]{1,0:T(8,128)S(1)} %get-tuple-element.20) | data formatting | bytes 1048576
  (28 shorter events, 0.2 us)
Async XLA Ops:
  0.6 10.5 %copy-start.9 = (s32[4096,2]{0,1:T(2,128)S(1)}, s32[4096,2]{0,1:T(2,128)}, u32[]{:S(2)}) copy-start(s32[4096,2]{0,1:T(2,128)} %param.21) | copy-start | bytes 98308
  0.6 10.6 %copy-start.10 = (s32[32]{0:T(128)S(1)}, s32[32]{0:T(128)}, u32[]{:S(2)}) copy-start(s32[32]{0:T(128)} %param.20) | copy-start | bytes 388
  3.8 20.5 %all-to-all-start = ((bf16[32,48,128]{2,1,0:T(8,128)(2,1)}), bf16[32,48,128]{2,1,0:T(8,128)(2,1)S(1)}, u32[]{:S(2)}, u32[]{:S(2)}) async-start(bf16[32,48,128]{2,1,0:T(8,128)(2,1)} %copy.22), calls=%async_computation | async-start | bytes 786432 | tf_op jit(solution)/shard_map/all_to_all | solution.py:370
  25.3 1.0 %copy-start = (bf16[32,4096]{1,0:T(8,128)(2,1)S(1)}, bf16[32,4096]{1,0:T(8,128)(2,1)}, u32[]{:S(2)}) copy-start(bf16[32,4096]{1,0:T(8,128)(2,1)} %rest_1_.1) | copy-start | bytes 786436
  25.3 1.1 %copy-start.1 = (f32[6,8,16,128]{3,2,1,0:T(8,128)S(1)}, f32[6,8,16,128]{3,2,1,0:T(8,128)}, u32[]{:S(2)}) copy-start(f32[6,8,16,128]{3,2,1,0:T(8,128)} %stress.1) | copy-start | bytes 1179652
  25.3 1.2 %copy-start.2 = (bf16[12,8,16,128]{3,2,1,0:T(8,128)(2,1)S(1)}, bf16[12,8,16,128]{3,2,1,0:T(8,128)(2,1)}, u32[]{:S(2)}) copy-start(bf16[12,8,16,128]{3,2,1,0:T(8,128)(2,1)} %strain.1) | copy-start | bytes 1179652
  25.3 1.2 %copy-start.3 = (f32[3,8,16,128]{3,2,1,0:T(8,128)S(1)}, f32[3,8,16,128]{3,2,1,0:T(8,128)}, u32[]{:S(2)}) copy-start(f32[3,8,16,128]{3,2,1,0:T(8,128)} %velocity.1) | copy-start | bytes 589828
  25.4 1.2 %copy-start.4 = (f32[8,16,128]{2,1,0:T(8,128)S(1)}, f32[8,16,128]{2,1,0:T(8,128)}, u32[]{:S(2)}) copy-start(f32[8,16,128]{2,1,0:T(8,128)} %lame_first.1) | copy-start | bytes 196612
  25.4 1.2 %copy-start.5 = (f32[8,16,128]{2,1,0:T(8,128)S(1)}, f32[8,16,128]{2,1,0:T(8,128)}, u32[]{:S(2)}) copy-start(f32[8,16,128]{2,1,0:T(8,128)} %shear_modulus.1) | copy-start | bytes 196612
  25.4 1.2 %copy-start.6 = (f32[8,16,128]{2,1,0:T(8,128)S(1)}, f32[8,16,128]{2,1,0:T(8,128)}, u32[]{:S(2)}) copy-start(f32[8,16,128]{2,1,0:T(8,128)} %buoyancy.1) | copy-start | bytes 196612
  25.4 1.2 %copy-start.7 = (f32[8,16,128]{2,1,0:T(8,128)S(1)}, f32[8,16,128]{2,1,0:T(8,128)}, u32[]{:S(2)}) copy-start(f32[8,16,128]{2,1,0:T(8,128)} %lame_accum.1) | copy-start | bytes 196612
  25.4 1.2 %copy-start.8 = (f32[8,16,128]{2,1,0:T(8,128)S(1)}, f32[8,16,128]{2,1,0:T(8,128)}, u32[]{:S(2)}) copy-start(f32[8,16,128]{2,1,0:T(8,128)} %shear_accum.1) | copy-start | bytes 196612

commit v4 on v3

--- a/solution.py
+++ b/solution.py
@@ -146,10 +146,7 @@
             normed = residuals[:, part * width : (part + 1) * width].astype(jnp.float32) * scale
             total = total + normed * back_rows[part]
         corr_sum = jnp.sum(total, axis=1, keepdims=True) * (1.0 / (devices * width))
-        for part in range(devices):
-            normed = residuals[:, part * width : (part + 1) * width].astype(jnp.float32) * scale
-            last = back_rows[part] - corr_sum * normed
-            adjoint[:, part * width : (part + 1) * width] = last
+        last = back_rows[devices - 1] - corr_sum * normed
         station = lax.broadcasted_iota(jnp.int32, last.shape, 0)
         lane = lax.broadcasted_iota(jnp.int32, last.shape, 1)
         depth = lax.broadcasted_iota(jnp.int32, hits.shape, 2)
@@ -160,6 +157,13 @@
             row = jnp.sum(jnp.where(station == lane, column, 0.0), axis=0, keepdims=True)
             cells = jnp.sum(hits[...] * row[None], axis=2, keepdims=True)
             fields[window_step] = jnp.where(depth == 0, cells, 0.0)
+        return corr_sum * scale
+
+    def write_adjoint(own_weight):
+        width = back_rows.shape[2]
+        for part in range(devices):
+            own = residuals[:, part * width : (part + 1) * width].astype(jnp.float32)
+            adjoint[:, part * width : (part + 1) * width] = back_rows[part] - own_weight * own
 
     def copy_of(phase, side):
         axis, step = sides[side]
@@ -233,12 +237,14 @@
         for part in range(3):
             velocity_out[part] = motion[part] + time_step * buoyancy[...] * forces[part]
         if fused and window_step == 0:
-            finish_sums()
+            own_weight = finish_sums()
             velocity_out[2] += time_step * buoyancy[...] * fields[0]
         phase += 1
         moved = [velocity_out[part] for part in range(3)]
         fill(phase, moved, moved)
         send(phase)
+        if fused and window_step == 0:
+            write_adjoint(own_weight)
         rate_third = third_back(moved[2])
         shear_two = third_ahead(moved[0])
         shear_three = third_ahead(moved[1])

time: 59.9 us -> 59.9 us (level)
  no operation moved by 1% of the time
where the time goes in v4:
time: 59.9 us; the launch traced here: 59.6 us
  Pallas kernels  29.5 us (49%)
  waiting for transfers between devices  9.19 us (15%)
  starting transfers between devices  7.3 us (12%)
  local copies, waits for them, and re-layouts  5.92 us (10%)
  matrix products  5.12 us (9%)
  other arithmetic  1.71 us (3%)
  between operations  0.87 us (1%)
    pallas_call x1, Pallas kernels, run_window(): pl.pallas_call(functools.partial(stencil_kernel, counts, fused), out_shap...  29.5 us
    all_to_all x1, waiting for transfers between devices, shard_sums(): lax.all_to_all(payload, axes, split_axis=0, concat_axis=0, tiled=True)  9.19 us
    all_to_all x1, starting transfers between devices, shard_sums(): lax.all_to_all(payload, axes, split_axis=0, concat_axis=0, tiled=True)  7.3 us
    unnamed x29, local copies, waits for them, and re-layouts  4.91 us
    dot_general x1, matrix products, partner_sums(): jnp.einsum('bpj,bpt->bjt', first_hot, second_hot, preferred_element_type=...  3.66 us
  transfers between devices with their start and end apart: 1, of which 1 were waited for; matrix products, arithmetic and copies ran while one was open for 7% of the time, Pallas kernels for 0%

profile of v4, /device:TPU:0, one launch (start us, length us, event | category | flops | bytes accessed | tf_op | source)
XLA Modules:
  0.0 59.6 jit_solution(1410579389486176008)
XLA Ops:
  0.7 1.1 %multiply_reduce_fusion = f32[32]{0:T(128)S(1)} fusion(bf16[32,4096]{1,0:T(8,128)(2,1)} %rest_1_.1), kind=kLoop, calls=%fused_computation.11 | loop fusion | flops 393184 | bytes 262272 | tf_op jit(solution)/shard_map/reduce_sum | solution.py:365
  1.8 1.0 %copy.25 = bf16[4,8,32,128]{3,2,1,0:T(8,128)(2,1)S(1)} copy(bf16[4,8,32,128]{3,1,2,0:T(8,128)(2,1)} %bitcast.27) | data formatting | bytes 524288
  2.9 0.9 %copy.22 = bf16[32,48,128]{2,1,0:T(8,128)(2,1)} copy(bf16[32,48,128]{2,0,1:T(8,128)(2,1)S(1)} %pad_maximum_fusion.1) | data formatting | bytes 786432 | tf_op jit(solution)/shard_map/concatenate | solution.py:369
  3.8 7.3 %all-to-all-start = ((bf16[32,48,128]{2,1,0:T(8,128)(2,1)}), bf16[32,48,128]{2,1,0:T(8,128)(2,1)S(1)}, u32[]{:S(2)}, u32[]{:S(2)}) async-start(bf16[32,48,128]{2,1,0:T(8,128)(2,1)} %copy.22), calls=%async_computation | async-start | bytes 786432 | tf_op jit(solution)/shard_map/all_to_all | solution.py:376
  11.1 0.1 copy.23.rest_2_
  11.2 0.1 fusion.7
  11.3 0.1 compare_convert_fusion.rest_3_
  11.4 3.7 %fusion.2 = bf16[32,32,1024]{2,1,0:T(8,128)(2,1)S(1)} fusion(s32[32,128]{1,0:T(8,128)S(1)} %get-tuple-element.8, s32[32,128]{1,0:T(8,128)S(1)} %get-tuple-element.7), kind=kOutput, calls=%fused_computation.3 | convolution fusion | flops 273809408 | bytes 2129920 | tf_op jit(solution)/shard_map/bpj,bpt->bjt/dot_general | solution.py:345
  15.1 9.2 %all-to-all-done = bf16[32,48,128]{2,1,0:T(8,128)(2,1)S(1)} async-done(((bf16[32,48,128]{2,1,0:T(8,128)(2,1)}), bf16[32,48,128]{2,1,0:T(8,128)(2,1)S(1)}, u32[]{:S(2)}, u32[]{:S(2)}) %all-to-all-start) | async-done | bytes 393248 | tf_op jit(solution)/shard_map/all_to_all | solution.py:376
  24.3 0.2 convert_multiply_fusion
  24.5 0.1 reduce-precision_convert_fusion
  24.6 0.7 %fusion.4 = f32[1024,256]{1,0:T(8,128)S(1)} fusion(bf16[1024,1024]{1,0:T(8,128)(2,1)S(1)} %bitcast.33, bf16[1024,128]{1,0:T(8,128)(2,1)S(1)} %get-tuple-element.6, bf16[1024,128]{1,0:T(8,128)(2,1)S(1)} %get-tuple-element.5), kind=kOutput, calls=%fused_computation.14 | convolution fusion | flops 537919488 | bytes 3670016 | tf_op jit(solution)/shard_map/dot_general | solution.py:351
  25.4 0.7 %convolution_add_fusion = f32[1024,256]{1,0:T(8,128)S(1)} fusion(f32[1024,256]{1,0:T(8,128)S(1)} %fusion.4, bf16[1024,1024]{1,0:T(8,128)(2,1)S(1)} %bitcast.34, bf16[1024,128]{1,0:T(8,128)(2,1)S(1)} %get-tuple-element.6, bf16[1024,128]{1,0:T(8,128)(2,1)S(1)} %get-tuple-element.5), kind=kOutput, calls=%fused_computation.4 | convolution fusion | flops 538181632 | bytes 4718592 | tf_op jit(solution)/shard_map/dot_general | solution.py:353
  26.2 0.1 slice_add_fusion
  26.2 0.0 copy-done
  26.3 0.1 copy-done.1
  26.4 0.1 copy-done.2
  26.5 0.0 copy-done.3
  26.6 29.5 %shard_map.146 = (f32[3,8,16,128]{3,2,1,0:T(8,128)S(1)}, f32[6,8,16,128]{3,2,1,0:T(8,128)S(1)}, f32[8,16,128]{2,1,0:T(8,128)S(1)}, f32[8,16,128]{2,1,0:T(8,128)S(1)}, f32[32,4096]{1,0:T(8,128)S(1)}) custom-call(f32[3,8,16,128]{3,2,1,0:T(8,128)S(1)} %copy-done.3, f32[6,8,16,128]{3,2,1,0:T(8,128)S(1)} %copy-done.1, f32[8,16,128]{2,1,0:T(8,128)S(1)} %copy-done.4, ...), custom_call_target="tpu_custom_call" | custom-call | tf_op jit(solution)/shard_map/pallas_call | solution.py:315
  56.1 0.7 %copy.33 = f32[3,8,16,128]{3,2,1,0:T(8,128)} copy(f32[3,8,16,128]{3,2,1,0:T(8,128)S(1)} %get-tuple-element.16) | data formatting | bytes 393216
  56.8 0.7 %copy.34 = f32[6,8,16,128]{3,2,1,0:T(8,128)} copy(f32[6,8,16,128]{3,2,1,0:T(8,128)S(1)} %get-tuple-element.17) | data formatting | bytes 786432
  57.6 0.6 %copy.35 = f32[8,16,128]{2,1,0:T(8,128)} copy(f32[8,16,128]{2,1,0:T(8,128)S(1)} %get-tuple-element.18) | data formatting | bytes 131072
  58.2 0.6 %copy.36 = f32[8,16,128]{2,1,0:T(8,128)} copy(f32[8,16,128]{2,1,0:T(8,128)S(1)} %get-tuple-element.19) | data formatting | bytes 131072
  58.8 0.8 %copy.37 = f32[32,4096]{1,0:T(8,128)} copy(f32[32,4096]{1,0:T(8,128)S(1)} %get-tuple-element.20) | data formatting | bytes 1048576
  (28 shorter events, 0.2 us)
Async XLA Ops:
  0.6 10.5 %copy-start.9 = (s32[4096,2]{0,1:T(2,128)S(1)}, s32[4096,2]{0,1:T(2,128)}, u32[]{:S(2)}) copy-start(s32[4096,2]{0,1:T(2,128)} %param.21) | copy-start | bytes 98308
  0.6 10.6 %copy-start.10 = (s32[32]{0:T(128)S(1)}, s32[32]{0:T(128)}, u32[]{:S(2)}) copy-start(s32[32]{0:T(128)} %param.20) | copy-start | bytes 388
  3.8 20.5 %all-to-all-start = ((bf16[32,48,128]{2,1,0:T(8,128)(2,1)}), bf16[32,48,128]{2,1,0:T(8,128)(2,1)S(1)}, u32[]{:S(2)}, u32[]{:S(2)}) async-start(bf16[32,48,128]{2,1,0:T(8,128)(2,1)} %copy.22), calls=%async_computation | async-start | bytes 786432 | tf_op jit(solution)/shard_map/all_to_all | solution.py:376
  25.3 1.0 %copy-start = (bf16[32,4096]{1,0:T(8,128)(2,1)S(1)}, bf16[32,4096]{1,0:T(8,128)(2,1)}, u32[]{:S(2)}) copy-start(bf16[32,4096]{1,0:T(8,128)(2,1)} %rest_1_.1) | copy-start | bytes 786436
  25.3 1.1 %copy-start.1 = (f32[6,8,16,128]{3,2,1,0:T(8,128)S(1)}, f32[6,8,16,128]{3,2,1,0:T(8,128)}, u32[]{:S(2)}) copy-start(f32[6,8,16,128]{3,2,1,0:T(8,128)} %stress.1) | copy-start | bytes 1179652
  25.3 1.2 %copy-start.2 = (bf16[12,8,16,128]{3,2,1,0:T(8,128)(2,1)S(1)}, bf16[12,8,16,128]{3,2,1,0:T(8,128)(2,1)}, u32[]{:S(2)}) copy-start(bf16[12,8,16,128]{3,2,1,0:T(8,128)(2,1)} %strain.1) | copy-start | bytes 1179652
  25.3 1.2 %copy-start.3 = (f32[3,8,16,128]{3,2,1,0:T(8,128)S(1)}, f32[3,8,16,128]{3,2,1,0:T(8,128)}, u32[]{:S(2)}) copy-start(f32[3,8,16,128]{3,2,1,0:T(8,128)} %velocity.1) | copy-start | bytes 589828
  25.4 1.2 %copy-start.4 = (f32[8,16,128]{2,1,0:T(8,128)S(1)}, f32[8,16,128]{2,1,0:T(8,128)}, u32[]{:S(2)}) copy-start(f32[8,16,128]{2,1,0:T(8,128)} %lame_first.1) | copy-start | bytes 196612
  25.4 1.2 %copy-start.5 = (f32[8,16,128]{2,1,0:T(8,128)S(1)}, f32[8,16,128]{2,1,0:T(8,128)}, u32[]{:S(2)}) copy-start(f32[8,16,128]{2,1,0:T(8,128)} %shear_modulus.1) | copy-start | bytes 196612
  25.4 1.2 %copy-start.6 = (f32[8,16,128]{2,1,0:T(8,128)S(1)}, f32[8,16,128]{2,1,0:T(8,128)}, u32[]{:S(2)}) copy-start(f32[8,16,128]{2,1,0:T(8,128)} %buoyancy.1) | copy-start | bytes 196612
  25.4 1.2 %copy-start.7 = (f32[8,16,128]{2,1,0:T(8,128)S(1)}, f32[8,16,128]{2,1,0:T(8,128)}, u32[]{:S(2)}) copy-start(f32[8,16,128]{2,1,0:T(8,128)} %lame_accum.1) | copy-start | bytes 196612
  25.4 1.2 %copy-start.8 = (f32[8,16,128]{2,1,0:T(8,128)S(1)}, f32[8,16,128]{2,1,0:T(8,128)}, u32[]{:S(2)}) copy-start(f32[8,16,128]{2,1,0:T(8,128)} %shear_accum.1) | copy-start | bytes 196612
